TPU v7x, 32 devices: a whole 2x2x4 slice. The times are simulated.
32 devices in a mesh: dp: 4 (over y, x), mx: 4 (over z), my: 2 (over core).
Axes of the slice: x: 2, y: 2, z: 4, core: 2. Of those that a mesh axis runs over, the one named last changes fastest.
Arguments:
- block_entry_rows: bfloat16 [8192, 768], P(('dp', 'my'), 'mx'), may hold values from -6 to 6
- cotangent: bfloat16 [8192, 768], P(('dp', 'my'), 'mx'), may hold values from -6 to 6
- gain_one: float32 [768], replicated, may hold values from 0.5 to 1.5
- w_qkv: bfloat16 [768, 3, 768], P('my', None, 'mx'), may hold values from -0.21875 to 0.21875
- w_out_attn: bfloat16 [768, 768], P('mx', 'my'), may hold values from -3.5 to 3.5
- rel_bias: float32 [12, 32], replicated, may hold values from -4 to 4
- gain_two: float32 [768], replicated, may hold values from 0.5 to 1.5
- router: bfloat16 [768, 8], replicated, may hold values from -0.21875 to 0.21875
- w_in: bfloat16 [8, 768, 3072], P('dp', 'my', 'mx'), may hold values from -0.21875 to 0.21875
- w_out: bfloat16 [8, 3072, 768], P('dp', 'mx', 'my'), may hold values from -0.109375 to 0.109375
- routes: int32 [8192, 2], P(('dp', 'my')), may hold values from 0 to 7, all different within a row
- slot_order: int32 [8, 2048], P(('dp', 'my')), may hold values from 0 to 2047, each once within a row
- cont_ids: int32 [4, 1024], P('dp'), may hold values from 0 to 7, never falling along the last dimension, each value on 1 to 256 neighbouring positions
Outputs:
- block_output: float32 [8192, 768], P(('dp', 'my'), 'mx')
- d_x: float32 [8192, 768], P(('dp', 'my'), 'mx')
- d_w_qkv: float32 [768, 3, 768], P('my', None, 'mx')
- d_w_out_attn: float32 [768, 768], P('mx', 'my')
- d_rel_bias: float32 [12, 32], replicated
- d_gain_one: float32 [768], replicated
- d_gain_two: float32 [768], replicated
- d_router: float32 [768, 8], replicated
- d_w_in: float32 [8, 768, 3072], P('dp', 'my', 'mx')
- d_w_out: float32 [8, 3072, 768], P('dp', 'mx', 'my')
Inputs may be any that keep to these rules, and one draw needn't show every extreme that they name: `routes`: each token names two different experts. `slot_order`: each row is an ordering of 0 to 2047, each number once. `cont_ids`: never falling along a row; every continuation has 1 to 256 tokens, and one has exactly 256.
All inputs are finite; a program needn't handle non-finite values.
Results may differ from a plain program's by a relative error of at most 0.022.
Values may be sent and summed in bfloat16 or wider, within the bound.
No kernel may reach another device: no remote copies, remote signals or barrier semaphores. Data moves between devices by JAX's collectives and lax.ppermute only.
A program may use at most 256 MiB of HBM per device.

v0:
```python
import jax
import jax.numpy as jnp
from jax import lax
from jax.sharding import PartitionSpec as P

MODEL_WIDTH = 768
HEAD = 64
NB = 32
BUCKET = 32


EPS = 1e-06
NEG = -1e30


def from_behind(x, axis, by):
    count = lax.axis_size(axis)
    pairs = [(i, i + by) for i in range(count) if 0 <= i + by < count]
    return lax.ppermute(x, axis, pairs)


def feature_gather(values):
    return lax.all_gather(values, "mx", axis=1, tiled=True)


def feature_sum(values):
    return lax.psum_scatter(values, "mx", scatter_dimension=1, tiled=True)


def row_dot_total(values):
    return lax.psum(values, "mx")


def expert_swap(values):
    return lax.all_to_all(values, "dp", split_axis=0, concat_axis=0, tiled=True)


def slot_table(route_rows, order, experts, cap_rows):
    flat = route_rows.reshape(-1)
    ranked = flat[order]
    one_hot = (ranked[:, None] == jnp.arange(experts, dtype=jnp.int32)[None, :]).astype(jnp.int32)
    before = jnp.cumsum(one_hot, axis=0) - one_hot
    rank_sorted = jnp.sum(before * one_hot, axis=1)
    ranking = jnp.zeros_like(flat).at[order].set(rank_sorted)
    kept = ranking < cap_rows
    slot_id = flat * cap_rows + jnp.minimum(ranking, cap_rows - 1)
    target = jnp.where(kept, slot_id, experts * cap_rows)
    source = (
        jnp.zeros((experts * cap_rows,), jnp.int32)
        .at[target]
        .set(jnp.arange(flat.shape[0], dtype=jnp.int32), mode="drop")
    )
    filled = jnp.zeros((experts * cap_rows,), jnp.int32).at[target].set(1, mode="drop")
    return (slot_id, kept, source, filled)


def layout(seg_ids, is_cont, tok_len):
    index = jnp.arange(tok_len, dtype=jnp.int32)
    same_seg = seg_ids[:, None] == seg_ids[None, :]
    first_pos = jnp.min(jnp.where(same_seg, index[None, :], tok_len), axis=1)
    own_pos = jnp.where(is_cont, tok_len + index - first_pos, index)
    own_seg = jnp.where(is_cont, seg_ids, -1)
    own_index = index + jnp.where(is_cont, tok_len, 0)
    key_pos = jnp.concatenate([index, own_pos])
    key_seg = jnp.concatenate([jnp.full((tok_len,), -1, jnp.int32), own_seg])
    key_index = jnp.concatenate([index, own_index])
    key_live = jnp.concatenate([jnp.full((tok_len,), is_cont), jnp.full((tok_len,), True)])
    return (own_pos, own_seg, own_index, (key_pos, key_seg, key_index, key_live))


def block_scores(
    query_block, keys_all, bias_parts, query_pos, query_seg, query_index, geometry, tok_len
):
    key_pos, key_seg, key_index, key_live = geometry
    bias_high, bias_rest = bias_parts
    raw = jnp.einsum(
        "qhd,khd->hqk", query_block, keys_all, preferred_element_type=jnp.float32
    ) * HEAD ** (-0.5)
    distance = jnp.maximum(query_pos[:, None] - key_pos[None, :], 0)
    bucket = jnp.minimum(distance // BUCKET, NB - 1)
    bucket_hot = (bucket[:, :, None] == jnp.arange(NB, dtype=jnp.int32)[None, None, :]).astype(
        jnp.bfloat16
    )
    raw = raw + jnp.einsum("qkb,hb->hqk", bucket_hot, bias_high, preferred_element_type=jnp.float32)
    raw = raw + jnp.einsum("qkb,hb->hqk", bucket_hot, bias_rest, preferred_element_type=jnp.float32)
    allowed = (
        key_live[None, :]
        & (key_index[None, :] <= query_index[:, None])
        & ((key_index[None, :] < tok_len) | (key_seg[None, :] == query_seg[:, None]))
    )
    return (jnp.where(allowed[None], raw, NEG), bucket_hot)


def root_mean_square_pullback(normalized_gradient, local_gain, unit_scaled_input, inverse_norm):
    unit_scaled_gradient = normalized_gradient * local_gain
    norm_gain_gradient = jnp.sum(normalized_gradient * unit_scaled_input, axis=0)
    normalized_dot_product = (
        row_dot_total(jnp.sum(unit_scaled_gradient * unit_scaled_input, axis=1, keepdims=True))
        / MODEL_WIDTH
    )
    return (
        inverse_norm * (unit_scaled_gradient - unit_scaled_input * normalized_dot_product),
        norm_gain_gradient,
    )


def body(
    block_entry_rows,
    cotangent,
    gain_one,
    w_qkv,
    w_out_attn,
    rel_bias,
    gain_two,
    router,
    w_in,
    w_out,
    routes,
    slot_order,
    cont_ids,
):
    tok_len = block_entry_rows.shape[0]
    feat_local = block_entry_rows.shape[1]
    feat_index = lax.axis_index("mx")
    feat_start = feat_index * feat_local
    is_cont = lax.axis_index("my") == 1
    experts = router.shape[1]
    per_dev = w_in.shape[0]
    owners = experts // per_dev
    cap_rows = 2 * tok_len // experts
    inner_local = w_qkv.shape[2]
    heads_local = inner_local // HEAD
    block_rows = min(512, tok_len)
    block_count = tok_len // block_rows
    qkv_full, proj_full, win_full, wout_full = (
        lax.all_gather(w_qkv, "my", axis=0, tiled=True),
        lax.all_gather(w_out_attn, "my", axis=1, tiled=True),
        lax.all_gather(w_in, "my", axis=1, tiled=True),
        lax.all_gather(w_out, "my", axis=2, tiled=True),
    )
    qkv_flat = qkv_full.reshape(qkv_full.shape[0], 3 * inner_local)
    x_full = feature_gather(block_entry_rows).astype(jnp.float32)
    first_inverse_norm = lax.rsqrt(jnp.mean(x_full * x_full, axis=1, keepdims=True) + EPS)
    normed_one = (x_full * first_inverse_norm * gain_one).astype(jnp.bfloat16)
    projected = jnp.dot(normed_one, qkv_flat, preferred_element_type=jnp.float32).astype(
        jnp.bfloat16
    )
    queries = projected[:, :inner_local].reshape(tok_len, heads_local, HEAD)
    keys_own = projected[:, inner_local : 2 * inner_local].reshape(tok_len, heads_local, HEAD)
    vals_own = projected[:, 2 * inner_local :].reshape(tok_len, heads_local, HEAD)
    keys_prev, vals_prev = from_behind((keys_own, vals_own), "my", 1)
    keys_all = jnp.concatenate([keys_prev, keys_own], axis=0)
    vals_all = jnp.concatenate([vals_prev, vals_own], axis=0)
    own_pos, own_seg, own_index, geometry = layout(cont_ids[0], is_cont, tok_len)
    bias_local = lax.dynamic_slice_in_dim(rel_bias, feat_index * heads_local, heads_local, 0)
    bias_high = bias_local.astype(jnp.bfloat16)
    bias_rest = (bias_local - bias_high.astype(jnp.float32)).astype(jnp.bfloat16)
    bias_parts = (bias_high, bias_rest)
    query_blocks = queries.reshape(block_count, block_rows, heads_local, HEAD)
    pos_blocks = own_pos.reshape(block_count, block_rows)
    seg_blocks = own_seg.reshape(block_count, block_rows)
    index_blocks = own_index.reshape(block_count, block_rows)

    def forward_block(packed):
        query_block, query_pos, query_seg, query_index = packed
        scores, bucket_hot = block_scores(
            query_block, keys_all, bias_parts, query_pos, query_seg, query_index, geometry, tok_len
        )
        row_top = jnp.max(scores, axis=-1, keepdims=True)
        exp_terms = jnp.exp(scores - row_top)
        row_sum = jnp.sum(exp_terms, axis=-1, keepdims=True)
        probs = (exp_terms / row_sum).astype(jnp.bfloat16)
        block_out = jnp.einsum("hqk,khd->qhd", probs, vals_all, preferred_element_type=jnp.float32)
        return (block_out.astype(jnp.bfloat16), (row_top + jnp.log(row_sum))[..., 0])

    mixed_blocks, log_sums = lax.map(
        forward_block, (query_blocks, pos_blocks, seg_blocks, index_blocks)
    )
    mixed = mixed_blocks.reshape(tok_len, inner_local)
    branch = feature_sum(jnp.dot(mixed, proj_full, preferred_element_type=jnp.float32))
    hidden_activation = block_entry_rows.astype(jnp.float32) + branch
    second_inverse_norm = lax.rsqrt(
        row_dot_total(jnp.sum(hidden_activation * hidden_activation, axis=1, keepdims=True))
        / MODEL_WIDTH
        + EPS
    )
    local_gain_second = lax.dynamic_slice_in_dim(gain_two, feat_start, feat_local, 0)
    second_unit_scaled = hidden_activation * second_inverse_norm
    second_normalized = (second_unit_scaled * local_gain_second).astype(jnp.bfloat16)
    normed_full = feature_gather(second_normalized)
    logits = jnp.dot(normed_full, router, preferred_element_type=jnp.float32)
    route_hot = routes[:, :, None] == jnp.arange(experts, dtype=jnp.int32)[None, None, :]
    chosen = jnp.sum(jnp.where(route_hot, logits[:, None, :], 0.0), axis=2)
    gates = jax.nn.softmax(chosen, axis=1)
    slot_id, kept, source, filled = slot_table(routes, slot_order[0], experts, cap_rows)
    kept_rows = kept.reshape(tok_len, 2).astype(jnp.float32)
    slot_rows = slot_id.reshape(tok_len, 2)
    fill_mask = filled[:, None].astype(jnp.bfloat16)
    outgoing = jnp.take(second_normalized, source // 2, axis=0) * fill_mask
    arrived = expert_swap(outgoing.reshape(owners, per_dev * cap_rows, feat_local))
    rows_full = feature_gather(arrived.reshape(-1, feat_local)).reshape(
        owners, per_dev, cap_rows, -1
    )
    pre_act = jnp.einsum("sjcd,jdf->sjcf", rows_full, win_full, preferred_element_type=jnp.float32)
    activated = jax.nn.gelu(pre_act).astype(jnp.bfloat16)
    partial_out = jnp.einsum(
        "sjcf,jfd->sjcd", activated, wout_full, preferred_element_type=jnp.float32
    )
    expert_out = feature_sum(partial_out.reshape(owners * per_dev * cap_rows, -1)).astype(
        jnp.bfloat16
    )
    returned = expert_swap(expert_out.reshape(owners, per_dev * cap_rows, feat_local)).reshape(
        experts * cap_rows, feat_local
    )
    picked = jnp.take(returned, slot_rows, axis=0).astype(jnp.float32) * kept_rows[..., None]
    out_rows = hidden_activation + jnp.sum(gates[..., None] * picked, axis=1)
    grad_out = cotangent.astype(jnp.float32)
    gate_grad = row_dot_total(jnp.sum(grad_out[:, None, :] * picked, axis=2))
    back_rows = (
        (gates[..., None] * grad_out[:, None, :] * kept_rows[..., None])
        .astype(jnp.bfloat16)
        .reshape(2 * tok_len, feat_local)
    )
    back_sent = jnp.take(back_rows, source, axis=0) * fill_mask
    back_arrived = expert_swap(back_sent.reshape(owners, per_dev * cap_rows, feat_local))
    back_full = feature_gather(back_arrived.reshape(-1, feat_local)).reshape(
        owners, per_dev, cap_rows, -1
    )
    act_grad = jnp.einsum(
        "sjcd,jfd->sjcf", back_full, wout_full, preferred_element_type=jnp.float32
    )
    grad_wout = jnp.einsum(
        "sjcf,sjcd->jfd", activated, back_full, preferred_element_type=jnp.float32
    )
    gelu_value, gelu_pull = jax.vjp(jax.nn.gelu, pre_act)
    pre_grad = gelu_pull(act_grad)[0].astype(jnp.bfloat16)
    rows_part = jnp.einsum("sjcf,jdf->sjcd", pre_grad, win_full, preferred_element_type=jnp.float32)
    rows_grad = feature_sum(rows_part.reshape(owners * per_dev * cap_rows, -1)).astype(jnp.bfloat16)
    grad_win = jnp.einsum("sjcd,sjcf->jdf", rows_full, pre_grad, preferred_element_type=jnp.float32)
    rows_back = expert_swap(rows_grad.reshape(owners, per_dev * cap_rows, feat_local)).reshape(
        experts * cap_rows, feat_local
    )
    normalized_gradient = jnp.sum(
        jnp.take(rows_back, slot_rows, axis=0).astype(jnp.float32) * kept_rows[..., None], axis=1
    )
    gate_dot = jnp.sum(gates * gate_grad, axis=1, keepdims=True)
    chosen_grad = gates * (gate_grad - gate_dot)
    logit_grad = jnp.sum(jnp.where(route_hot, chosen_grad[:, :, None], 0.0), axis=1).astype(
        jnp.bfloat16
    )
    router_rows = lax.dynamic_slice_in_dim(router, feat_start, feat_local, 0)
    normalized_gradient = normalized_gradient + lax.dot_general(
        logit_grad, router_rows, (((1,), (1,)), ((), ())), preferred_element_type=jnp.float32
    )
    grad_router_rows = lax.dot_general(
        second_normalized, logit_grad, (((0,), (0,)), ((), ())), preferred_element_type=jnp.float32
    )
    second_norm_pullback, second_gain_gradient = root_mean_square_pullback(
        normalized_gradient, local_gain_second, second_unit_scaled, second_inverse_norm
    )
    hidden_grad = grad_out + second_norm_pullback
    hidden_full = feature_gather(hidden_grad.astype(jnp.bfloat16))
    mixed_grad = lax.dot_general(
        hidden_full, proj_full, (((1,), (1,)), ((), ())), preferred_element_type=jnp.float32
    ).astype(jnp.bfloat16)
    grad_proj = lax.dot_general(
        mixed, hidden_full, (((0,), (0,)), ((), ())), preferred_element_type=jnp.float32
    )
    grad_blocks = mixed_grad.reshape(block_count, block_rows, heads_local, HEAD)

    def backward_block(carry, packed):
        keys_grad, vals_grad, bias_grad = carry
        query_block, query_pos, query_seg, query_index, out_grad, log_sum = packed
        scores, bucket_hot = block_scores(
            query_block, keys_all, bias_parts, query_pos, query_seg, query_index, geometry, tok_len
        )
        probs = jnp.exp(scores - log_sum[..., None])
        prob_grad = jnp.einsum(
            "qhd,khd->hqk", out_grad, vals_all, preferred_element_type=jnp.float32
        )
        row_delta = jnp.sum(probs * prob_grad, axis=-1, keepdims=True)
        score_grad = (probs * (prob_grad - row_delta)).astype(jnp.bfloat16)
        query_grad = jnp.einsum(
            "hqk,khd->qhd", score_grad, keys_all, preferred_element_type=jnp.float32
        ) * HEAD ** (-0.5)
        keys_grad = keys_grad + jnp.einsum(
            "hqk,qhd->khd", score_grad, query_block, preferred_element_type=jnp.float32
        ) * HEAD ** (-0.5)
        vals_grad = vals_grad + jnp.einsum(
            "hqk,qhd->khd", probs.astype(jnp.bfloat16), out_grad, preferred_element_type=jnp.float32
        )
        bucket_sums = jnp.einsum(
            "hqk,qkb->hb", score_grad, bucket_hot, preferred_element_type=jnp.float32
        )
        return ((keys_grad, vals_grad, bias_grad + bucket_sums), query_grad)

    start_carry = (
        jnp.zeros((2 * tok_len, heads_local, HEAD), jnp.float32),
        jnp.zeros((2 * tok_len, heads_local, HEAD), jnp.float32),
        jnp.zeros((heads_local, NB), jnp.float32),
    )
    (keys_grad, vals_grad, bias_grad), query_grads = lax.scan(
        backward_block,
        start_carry,
        (query_blocks, pos_blocks, seg_blocks, index_blocks, grad_blocks, log_sums),
    )
    keys_back, vals_back = (
        from_behind(keys_grad[:tok_len].astype(jnp.bfloat16), "my", -1).astype(jnp.float32),
        from_behind(vals_grad[:tok_len].astype(jnp.bfloat16), "my", -1).astype(jnp.float32),
    )
    own_keys_grad = keys_grad[tok_len:] + keys_back
    own_vals_grad = vals_grad[tok_len:] + vals_back
    proj_grad = jnp.concatenate(
        [
            query_grads.reshape(tok_len, inner_local),
            own_keys_grad.reshape(tok_len, inner_local),
            own_vals_grad.reshape(tok_len, inner_local),
        ],
        axis=1,
    ).astype(jnp.bfloat16)
    grad_qkv = lax.dot_general(
        normed_one, proj_grad, (((0,), (0,)), ((), ())), preferred_element_type=jnp.float32
    ).reshape(qkv_full.shape[0], 3, inner_local)
    first_normalized_gradient = feature_sum(
        lax.dot_general(
            proj_grad, qkv_flat, (((1,), (1,)), ((), ())), preferred_element_type=jnp.float32
        )
    )
    local_gain_first = lax.dynamic_slice_in_dim(gain_one, feat_start, feat_local, 0)
    first_unit_scaled = block_entry_rows.astype(jnp.float32) * first_inverse_norm
    first_norm_pullback, first_gain_gradient = root_mean_square_pullback(
        first_normalized_gradient, local_gain_first, first_unit_scaled, first_inverse_norm
    )
    input_grad = hidden_grad + first_norm_pullback
    grad_qkv, grad_proj, grad_win, grad_wout = (
        lax.psum_scatter(
            grad_qkv.astype(jnp.bfloat16), "my", scatter_dimension=0, tiled=True
        ).astype(jnp.float32),
        lax.psum_scatter(
            grad_proj.astype(jnp.bfloat16), "my", scatter_dimension=1, tiled=True
        ).astype(jnp.float32),
        lax.psum_scatter(
            grad_win.astype(jnp.bfloat16), "my", scatter_dimension=1, tiled=True
        ).astype(jnp.float32),
        lax.psum_scatter(
            grad_wout.astype(jnp.bfloat16), "my", scatter_dimension=2, tiled=True
        ).astype(jnp.float32),
    )
    grad_qkv, grad_proj = (
        lax.psum(grad_qkv.astype(jnp.bfloat16), "dp").astype(jnp.float32),
        lax.psum(grad_proj.astype(jnp.bfloat16), "dp").astype(jnp.float32),
    )
    full_bias = lax.dynamic_update_slice_in_dim(
        jnp.zeros(rel_bias.shape, jnp.float32), bias_grad, feat_index * heads_local, 0
    )
    full_gain_one = lax.dynamic_update_slice_in_dim(
        jnp.zeros(gain_one.shape, jnp.float32), first_gain_gradient, feat_start, 0
    )
    full_gain_two = lax.dynamic_update_slice_in_dim(
        jnp.zeros(gain_two.shape, jnp.float32), second_gain_gradient, feat_start, 0
    )
    full_router = lax.dynamic_update_slice_in_dim(
        jnp.zeros(router.shape, jnp.float32), grad_router_rows, feat_start, 0
    )
    full_bias, full_gain_one, full_gain_two, full_router = lax.psum(
        (full_bias, full_gain_one, full_gain_two, full_router), ("dp", "mx", "my")
    )
    return (
        out_rows,
        input_grad,
        grad_qkv,
        grad_proj,
        full_bias,
        full_gain_one,
        full_gain_two,
        full_router,
        grad_win,
        grad_wout,
    )


def solution(mesh):
    return jax.shard_map(
        body,
        mesh=mesh,
        in_specs=(
            P(("dp", "my"), "mx"),
            P(("dp", "my"), "mx"),
            P(),
            P("my", None, "mx"),
            P("mx", "my"),
            P(),
            P(),
            P(),
            P("dp", "my", "mx"),
            P("dp", "mx", "my"),
            P(("dp", "my"), None),
            P(("dp", "my"), None),
            P("dp", None),
        ),
        out_specs=(
            P(("dp", "my"), "mx"),
            P(("dp", "my"), "mx"),
            P("my", None, "mx"),
            P("mx", "my"),
            P(),
            P(),
            P(),
            P(),
            P("dp", "my", "mx"),
            P("dp", "mx", "my"),
        ),
        check_vma=False,
    )
```

profile of v0, /device:TPU:0, one launch (start us, length us, event | category | flops | bytes accessed | tf_op | source)
XLA Modules:
  0.0 1479.6 jit_solution(3077496679853655198)
XLA Ops:
  13.8 35.6 %all-gather.8.cloned.1.call-done = bf16[1024,768]{0,1:T(8,128)(2,1)} async-done(((bf16[1024,192]{0,1:T(8,128)(2,1)}), bf16[1024,768]{0,1:T(8,128)(2,1)}) %all-gather.8.cloned.1.call-update) | async-done | bytes 1572880 | tf_op jit(solution)/shard_map/all_gather | solution.py:23
  60.2 184.3 %while.33 = (s32[]{:T(128)}, bf16[2,512,3,64]{1,3,2,0:T(8,128)(2,1)S(1)}, f32[2,3,512]{2,1,0:T(4,128)S(1)}, pred[2048]{0:T(1024)(128)(4,1)S(1)}, s32[2048]{0:T(1...) while((s32[]{:T(128)}, ...), condition=%wide.region_5.6_spmd, body=%wide.region_2.5_spmd.sunk | while | flops 1323401728 | bytes 155175504 | solution.py:176
  64.3 22.0 %fusion.188 = f32[512,2048,3]{1,2,0:T(4,128)} fusion(s32[512,2048]{1,0:T(8,128)S(1)} %fusion.186, bf16[3,32]{1,0:T(4,128)(2,1)S(1)} %get-tuple-element.1085), kind=kOutput, calls=%fused_computation.10.clone.1 | convolution fusion | flops 234881024 | bytes 16777408 | tf_op jit(solution)/shard_map/while/body/eval_jaxpr/qkb,hb->hqk/dot_general | solution.py:84
  86.4 22.0 %fusion.187 = f32[512,2048,3]{1,2,0:T(4,128)} fusion(s32[512,2048]{1,0:T(8,128)S(1)} %fusion.186, bf16[3,32]{1,0:T(4,128)(2,1)S(1)} %get-tuple-element.1086), kind=kOutput, calls=%fused_computation.9.clone.1 | convolution fusion | flops 234881024 | bytes 16777408 | tf_op jit(solution)/shard_map/while/body/eval_jaxpr/qkb,hb->hqk/dot_general | solution.py:85
  108.4 29.2 %fusion.189 = (f32[3,512]{1,0:T(4,128)S(1)}, f32[3,512,2048]{2,1,0:T(8,128)}) fusion(f32[512,2048,3]{1,2,0:T(4,128)} %fusion.187, f32[512,2048,3]{1,2,0:T(4,128)} %fusion.188, bf16[2048,3,64]{0,2,1:T(8,128)(2,1)S(1)} %get-tuple-element.1082, bf16[2,512,3,64]{1,3,2,0:T(8,128)(2,1)S(1)} %get-tuple-element.1081, s32[]{:T(128)S(6)} %copy.252, ...), kind=kOutput, calls=%fused_computation.235.clone.1 | convolution fusion | flops 418380288 | bytes 39786500 | tf_op jit(solution)/shard_map/while/body/eval_jaxpr/qhd,khd->hqk/dot_general | solution.py:76
  152.3 22.0 %fusion.188 = f32[512,2048,3]{1,2,0:T(4,128)} fusion(s32[512,2048]{1,0:T(8,128)S(1)} %fusion.186, bf16[3,32]{1,0:T(4,128)(2,1)S(1)} %get-tuple-element.1085), kind=kOutput, calls=%fused_computation.10.clone.1 | convolution fusion | flops 234881024 | bytes 16777408 | tf_op jit(solution)/shard_map/while/body/eval_jaxpr/qkb,hb->hqk/dot_general | solution.py:84
  174.3 22.0 %fusion.187 = f32[512,2048,3]{1,2,0:T(4,128)} fusion(s32[512,2048]{1,0:T(8,128)S(1)} %fusion.186, bf16[3,32]{1,0:T(4,128)(2,1)S(1)} %get-tuple-element.1086), kind=kOutput, calls=%fused_computation.9.clone.1 | convolution fusion | flops 234881024 | bytes 16777408 | tf_op jit(solution)/shard_map/while/body/eval_jaxpr/qkb,hb->hqk/dot_general | solution.py:85
  196.3 29.2 %fusion.189 = (f32[3,512]{1,0:T(4,128)S(1)}, f32[3,512,2048]{2,1,0:T(8,128)}) fusion(f32[512,2048,3]{1,2,0:T(4,128)} %fusion.187, f32[512,2048,3]{1,2,0:T(4,128)} %fusion.188, bf16[2048,3,64]{0,2,1:T(8,128)(2,1)S(1)} %get-tuple-element.1082, bf16[2,512,3,64]{1,3,2,0:T(8,128)(2,1)S(1)} %get-tuple-element.1081, s32[]{:T(128)S(6)} %copy.252, ...), kind=kOutput, calls=%fused_computation.235.clone.1 | convolution fusion | flops 418380288 | bytes 39786500 | tf_op jit(solution)/shard_map/while/body/eval_jaxpr/qhd,khd->hqk/dot_general | solution.py:76
  248.3 58.7 %reduce-scatter.19.cloned.1.call-done = f32[1024,192]{0,1:T(8,128)} async-done(((f32[1024,768]{0,1:T(8,128)}), f32[1024,192]{0,1:T(8,128)}) %reduce-scatter.19.cloned.1.call-update) | async-done | bytes 786448 | tf_op jit(solution)/shard_map/reduce_scatter | solution.py:27
  421.1 47.1 %all-gather.12.cloned.1.call-done = bf16[2048,768]{0,1:T(8,128)(2,1)} async-done(((bf16[2048,192]{0,1:T(8,128)(2,1)}), bf16[2048,768]{0,1:T(8,128)(2,1)}) %all-gather.12.cloned.1.call-update) | async-done | bytes 3145744 | tf_op jit(solution)/shard_map/all_gather | solution.py:23
  508.7 50.9 %all-gather.18.cloned.1.call-done = bf16[2048,768]{0,1:T(8,128)(2,1)} async-done(((bf16[2048,192]{0,1:T(8,128)(2,1)}), bf16[2048,768]{0,1:T(8,128)(2,1)}) %all-gather.18.cloned.1.call-update) | async-done | bytes 3145744 | tf_op jit(solution)/shard_map/all_gather | solution.py:23
  586.8 84.5 %reduce-scatter.25.cloned.1.call-done = f32[192,2048]{1,0:T(8,128)} async-done(((f32[768,2048]{1,0:T(8,128)}), f32[192,2048]{1,0:T(8,128)}) %reduce-scatter.25.cloned.1.call-update) | async-done | bytes 1572880
  678.8 106.1 %reduce-scatter.27.cloned.1.call-done = f32[192,2048]{1,0:T(8,128)} async-done(((f32[768,2048]{1,0:T(8,128)}), f32[192,2048]{1,0:T(8,128)}) %reduce-scatter.27.cloned.1.call-update) | async-done | bytes 1572880
  863.2 37.2 %all-gather.20.cloned.1.call-done = bf16[1024,768]{0,1:T(8,128)(2,1)} async-done(((bf16[1024,192]{0,1:T(8,128)(2,1)}), bf16[1024,768]{0,1:T(8,128)(2,1)}) %all-gather.20.cloned.1.call-update) | async-done | bytes 1572880 | tf_op jit(solution)/shard_map/all_gather | solution.py:23
  903.5 337.8 %while.34 = (s32[]{:T(128)}, f32[2048,3,64]{0,2,1:T(8,128)S(1)}, f32[2048,3,64]{0,2,1:T(8,128)}, f32[3,32]{1,0:T(4,128)S(1)}, bf16[2,512,3,64]{1,3,2,0:T(8,128)(...) while((s32[]{:T(128)}, f32[2048,3,64]{0,2,1:T(8,128)S(1)}, ...), condition=%wide.region_30.32_spmd.clone, body=%wide.region_28.31_spmd.clone.sunk | while | flops 2771354368 | bytes 358571680 | solution.py:302
  913.8 21.8 %fusion.207 = f32[512,2048,3]{0,2,1:T(4,128)} fusion(s32[512,2048]{0,1:T(8,128)S(1)} %fusion.205, bf16[3,32]{1,0:T(4,128)(2,1)S(1)} %get-tuple-element.1145), kind=kOutput, calls=%fused_computation.43.clone.1 | convolution fusion | flops 234881024 | bytes 16777408 | tf_op jit(solution)/shard_map/while/body/eval_jaxpr/qkb,hb->hqk/dot_general | solution.py:84
  953.0 22.9 %fusion.206 = f32[512,2048,3]{0,2,1:T(4,128)} fusion(s32[512,2048]{0,1:T(8,128)} %copy-done.7, bf16[3,32]{1,0:T(4,128)(2,1)S(1)} %get-tuple-element.1146), kind=kOutput, calls=%fused_computation.42.clone.1 | convolution fusion | flops 234881024 | bytes 16777408 | tf_op jit(solution)/shard_map/while/body/eval_jaxpr/qkb,hb->hqk/dot_general | solution.py:85
  1046.6 25.8 %fusion.210 = f32[3,32]{1,0:T(4,128)S(1)} fusion(bf16[3,512,2048]{1,0,2:T(4,128)(2,1)} %copy.245, s32[512,2048]{0,1:T(8,128)} %copy-done.7, f32[3,32]{1,0:T(4,128)S(1)} %get-tuple-element.1113, pred[]{:T(512)S(6)} %compare.15), kind=kOutput, calls=%fused_computation.72.clone.1 | convolution fusion | flops 234881216 | bytes 10486529 | tf_op jit(solution)/shard_map/while/body/eval_jaxpr/hqk,qkb->hb/dot_general | solution.py:292
  1082.4 21.8 %fusion.207 = f32[512,2048,3]{0,2,1:T(4,128)} fusion(s32[512,2048]{0,1:T(8,128)S(1)} %fusion.205, bf16[3,32]{1,0:T(4,128)(2,1)S(1)} %get-tuple-element.1145), kind=kOutput, calls=%fused_computation.43.clone.1 | convolution fusion | flops 234881024 | bytes 16777408 | tf_op jit(solution)/shard_map/while/body/eval_jaxpr/qkb,hb->hqk/dot_general | solution.py:84
  1121.6 22.9 %fusion.206 = f32[512,2048,3]{0,2,1:T(4,128)} fusion(s32[512,2048]{0,1:T(8,128)} %copy-done.7, bf16[3,32]{1,0:T(4,128)(2,1)S(1)} %get-tuple-element.1146), kind=kOutput, calls=%fused_computation.42.clone.1 | convolution fusion | flops 234881024 | bytes 16777408 | tf_op jit(solution)/shard_map/while/body/eval_jaxpr/qkb,hb->hqk/dot_general | solution.py:85
  1215.2 25.8 %fusion.210 = f32[3,32]{1,0:T(4,128)S(1)} fusion(bf16[3,512,2048]{1,0,2:T(4,128)(2,1)} %copy.245, s32[512,2048]{0,1:T(8,128)} %copy-done.7, f32[3,32]{1,0:T(4,128)S(1)} %get-tuple-element.1113, pred[]{:T(512)S(6)} %compare.15), kind=kOutput, calls=%fused_computation.72.clone.1 | convolution fusion | flops 234881216 | bytes 10486529 | tf_op jit(solution)/shard_map/while/body/eval_jaxpr/hqk,qkb->hb/dot_general | solution.py:292
  1309.5 46.0 %all-reduce.6.cloned.1.call-done = (bf16[384,3,192]{0,2,1:T(8,128)(2,1)}, bf16[192,384]{1,0:T(8,128)(2,1)}) async-done(((bf16[384,3,192]{0,2,1:T(8,128)(2,1)}, bf16[192,384]{1,0:T(8,128)(2,1)}), (bf16[384,3,192]{0,2,1:T(8,128)(2,1)}, bf16[192,384]{1,0:T(8,128)(2,1)})) %all-reduce.6.cloned.1.call-update) | async-done | bytes 589840 | tf_op jit(solution)/shard_map/psum | solution.py:350
  1359.1 58.9 %reduce-scatter.21.cloned.1.call-done = f32[1024,192]{0,1:T(8,128)} async-done(((f32[1024,768]{0,1:T(8,128)}), f32[1024,192]{0,1:T(8,128)}) %reduce-scatter.21.cloned.1.call-update) | async-done | bytes 786448 | tf_op jit(solution)/shard_map/reduce_scatter | solution.py:27
  1430.1 39.7 %all-reduce.2 = (f32[12,32]{1,0:T(8,128)}, f32[768]{0:T(1024)}, f32[768]{0:T(1024)}, f32[768,8]{0,1:T(8,128)}) all-reduce(f32[12,32]{1,0:T(8,128)S(1)} %dynamic_update_slice.33, f32[768]{0:T(1024)S(1)} %dynamic_update_slice.34, f32[768]{0:T(1024)S(1)} %dynamic_update_slice.35, ...), channel_id=1, replica_groups=mesh['dp'=4,'mx'=4,'my'=2] {'dp','mx','my'}, use_global_device_ids=true, to_apply=%region_38.40 | all-reduce | flops 8064 | bytes 64512 | tf_op jit(solution)/shard_map/psum | solution.py:365
  (407 shorter events, 602.7 us)
Async XLA Ops:
  7.2 42.2 %all-gather.8.cloned.1.call-start = ((), (), s32[]{:S(2)}) async-start(), calls=%async_computation.12 | async-start | bytes 1966080 | tf_op jit(solution)/shard_map/all_gather | solution.py:23
  7.9 299.1 %reduce-scatter.19.cloned.1.call-start = ((), (), s32[]{:S(2)}) async-start(), calls=%async_computation.13 | async-start | bytes 3932160 | tf_op jit(solution)/shard_map/reduce_scatter | solution.py:27
  54.5 5.6 collective-permute-start
  56.2 4.0 collective-permute-start.1
  247.5 129.2 %all-gather.10.cloned.1.call-start = ((), (), s32[]{:S(2)}) async-start(), calls=%async_computation.14 | async-start | bytes 1966080 | tf_op jit(solution)/shard_map/all_gather | solution.py:23
  248.3 613.7 %copy-start.52 = (f32[192]{0:T(256)}, f32[192]{0:T(256)S(1)}, u32[]{:S(2)}) copy-start(f32[192]{0:T(256)S(1)} %dynamic_slice.76) | copy-start | bytes 2308
  308.3 553.8 %copy-start.15 = (f32[1024,192]{0,1:T(8,128)}, f32[1024,192]{0,1:T(8,128)S(1)}, u32[]{:S(2)}) copy-start(f32[1024,192]{0,1:T(8,128)S(1)} %get-tuple-element.790) | copy-start | bytes 2359300
  319.7 148.6 %all-gather.12.cloned.1.call-start = ((), (), s32[]{:S(2)}) async-start(), calls=%async_computation.15 | async-start | bytes 3932160 | tf_op jit(solution)/shard_map/all_gather | solution.py:23
  407.9 71.4 %all-gather.14.cloned.1.call-start = ((), (), s32[]{:S(2)}) async-start(), calls=%async_computation.16 | async-start | bytes 3538944 | tf_op jit(solution)/shard_map/all_gather | solution.py:138
  408.5 84.3 %all-gather.16.cloned.1.call-start = ((), (), s32[]{:S(2)}) async-start(), calls=%async_computation.17 | async-start | bytes 3538944 | tf_op jit(solution)/shard_map/all_gather | solution.py:139
  409.1 150.6 %all-gather.18.cloned.1.call-start = ((), (), s32[]{:S(2)}) async-start(), calls=%async_computation.18 | async-start | bytes 3932160 | tf_op jit(solution)/shard_map/all_gather | solution.py:23
  421.1 250.3 %reduce-scatter.25.cloned.1.call-start = ((), (), s32[]{:S(2)}) async-start(), calls=%async_computation.22 | async-start | bytes 7864320
  508.7 276.3 %reduce-scatter.27.cloned.1.call-start = ((), (), s32[]{:S(2)}) async-start(), calls=%async_computation.23 | async-start | bytes 7864320
  674.2 115.3 %all-to-all-start.1 = ((bf16[4,512,192]{1,2,0:T(8,128)(2,1)}), bf16[4,512,192]{1,2,0:T(8,128)(2,1)}, u32[]{:S(2)}, u32[]{:S(2)}) async-start(bf16[4,512,192]{1,2,0:T(8,128)(2,1)} %copy.181), calls=%async_computation.2 | async-start | bytes 1572864 | tf_op jit(solution)/shard_map/all_to_all | solution.py:35
  789.5 20.0 %all-to-all-start.3 = ((bf16[4,512,192]{1,2,0:T(8,128)(2,1)}), bf16[4,512,192]{1,2,0:T(8,128)(2,1)}, u32[]{:S(2)}, u32[]{:S(2)}) async-start(bf16[4,512,192]{1,2,0:T(8,128)(2,1)} %copy.191), calls=%async_computation.4 | async-start | bytes 1572864 | tf_op jit(solution)/shard_map/all_to_all | solution.py:35
  793.7 106.7 %all-gather.20.cloned.1.call-start = ((), (), s32[]{:S(2)}) async-start(), calls=%async_computation.19 | async-start | bytes 1966080 | tf_op jit(solution)/shard_map/all_gather | solution.py:23
  863.1 423.5 %reduce-scatter.31.cloned.1.call-start = ((), (), s32[]{:S(2)}) async-start(), calls=%async_computation.25 | async-start | bytes 589824
  1243.4 10.7 collective-permute-start.3
  1245.5 9.7 collective-permute-start.2
  1254.0 34.5 %reduce-scatter.29.cloned.1.call-start = ((), (), s32[]{:S(2)}) async-start(), calls=%async_computation.24 | async-start | bytes 1474560
  1263.2 30.8 %reduce-scatter.33.cloned.1.call-start = ((), (), s32[]{:S(2)}) async-start(), calls=%async_computation.26 | async-start | bytes 3538944
  1279.5 25.1 %reduce-scatter.23.cloned.1.call-start = ((), (), s32[]{:S(2)}) async-start(), calls=%async_computation.21 | async-start | bytes 3538944 | tf_op jit(solution)/shard_map/reduce_scatter | solution.py:342
  1286.6 68.9 %all-reduce.6.cloned.1.call-start = ((), (), s32[]{:S(2)}) async-start(), calls=%async_computation.27 | async-start | bytes 1179648 | tf_op jit(solution)/shard_map/psum | solution.py:350
  1290.6 127.5 %reduce-scatter.21.cloned.1.call-start = ((), (), s32[]{:S(2)}) async-start(), calls=%async_computation.20 | async-start | bytes 3932160 | tf_op jit(solution)/shard_map/reduce_scatter | solution.py:27
  (73 other events, 3075.6 us)
Sparse Core Ops, SparseCore 0:
  9.6 39.7 all-gather.7
  247.5 59.4 reduce-scatter.18
  319.8 35.4 all-gather.9
  408.0 60.1 all-gather.11
  469.6 9.5 all-gather.13
  480.7 12.0 all-gather.15
  494.9 64.6 all-gather.17
  561.9 109.3 reduce-scatter.24
  673.7 111.2 reduce-scatter.26
  863.2 37.1 all-gather.19
  1254.1 8.9 reduce-scatter.30
  1265.3 9.6 reduce-scatter.28
  1279.7 11.0 reduce-scatter.32
  1293.5 11.0 reduce-scatter.22
  1308.1 47.3 all-reduce.5
  1357.7 60.2 reduce-scatter.20
where the time goes:
time: 1490 us; the launch traced here: 1480 us
  waiting for transfers between devices  543 us (36%)
  matrix products  417 us (28%)
  local copies, waits for them, and re-layouts  279 us (19%)
  blocking collectives  110 us (7%)
  other arithmetic  91 us (6%)
  starting transfers between devices  15.3 us (1%)
  between operations  15.3 us (1%)
    unnamed x21, waiting for transfers between devices  193 us
    all_gather x5, waiting for transfers between devices, feature_gather(): return lax.all_gather(values, 'mx', axis=1, tiled=True)  171 us
    reduce_scatter x2, waiting for transfers between devices, feature_sum(): return lax.psum_scatter(values, 'mx', scatter_dimension=1, tiled=True)  118 us
    dot_general x4, matrix products, block_scores(): jnp.einsum('qhd,khd->hqk', query_block, keys_all, preferred_element_type=...  97.2 us
    dot_general x4, matrix products, block_scores(): jnp.einsum('qkb,hb->hqk', bucket_hot, bias_rest, preferred_element_type=j...  89.8 us
    dot_general x4, matrix products, block_scores(): jnp.einsum('qkb,hb->hqk', bucket_hot, bias_high, preferred_element_type=j...  87.7 us
    dot_general x2, matrix products, backward_block(): jnp.einsum('hqk,qkb->hb', score_grad, bucket_hot, preferred_element_type=...  51.5 us
    psum x1, waiting for transfers between devices, body(): lax.psum(grad_qkv.astype(jnp.bfloat16), 'dp').astype(jnp.float32)  46 us
  transfers between devices with their start and end apart: 22, of which 12 were waited for; matrix products, arithmetic and copies ran while one was open for 14% of the time, Pallas kernels for 0%

commit v1 on v0

--- a/solution.py
+++ b/solution.py
@@ -1,6 +1,8 @@
 import jax
 import jax.numpy as jnp
 from jax import lax
+from jax.experimental import pallas as pl
+from jax.experimental.pallas import tpu as pltpu
 from jax.sharding import PartitionSpec as P
 
 MODEL_WIDTH = 768
@@ -24,7 +26,9 @@
 
 
 def feature_sum(values):
-    return lax.psum_scatter(values, "mx", scatter_dimension=1, tiled=True)
+    return lax.psum_scatter(
+        values.astype(jnp.bfloat16), "mx", scatter_dimension=1, tiled=True
+    ).astype(jnp.float32)
 
 
 def row_dot_total(values):
@@ -54,41 +58,269 @@
     return (slot_id, kept, source, filled)
 
 
-def layout(seg_ids, is_cont, tok_len):
-    index = jnp.arange(tok_len, dtype=jnp.int32)
-    same_seg = seg_ids[:, None] == seg_ids[None, :]
-    first_pos = jnp.min(jnp.where(same_seg, index[None, :], tok_len), axis=1)
-    own_pos = jnp.where(is_cont, tok_len + index - first_pos, index)
-    own_seg = jnp.where(is_cont, seg_ids, -1)
-    own_index = index + jnp.where(is_cont, tok_len, 0)
-    key_pos = jnp.concatenate([index, own_pos])
-    key_seg = jnp.concatenate([jnp.full((tok_len,), -1, jnp.int32), own_seg])
-    key_index = jnp.concatenate([index, own_index])
-    key_live = jnp.concatenate([jnp.full((tok_len,), is_cont), jnp.full((tok_len,), True)])
-    return (own_pos, own_seg, own_index, (key_pos, key_seg, key_index, key_live))
-
-
-def block_scores(
-    query_block, keys_all, bias_parts, query_pos, query_seg, query_index, geometry, tok_len
+SPAN = 256
+WIDE = pltpu.CompilerParams(vmem_limit_bytes=50 * 1024 * 1024)
+
+
+def iota(shape, dim):
+    return lax.broadcasted_iota(jnp.int32, shape, dim)
+
+
+def dot(a, b, dims=((1,), (0,))):
+    return lax.dot_general(a, b, (dims, ((), ())), preferred_element_type=jnp.float32)
+
+
+NT = ((1,), (1,))
+TN = ((0,), (0,))
+
+
+def fill_bias(near_ref, far_ref, table_ref):
+    low = (iota((BUCKET, SPAN), 1) & (BUCKET - 1)) >= iota((BUCKET, SPAN), 0)
+    for c in range(table_ref.shape[0] // BUCKET):
+        table_ref[c * BUCKET : (c + 1) * BUCKET, :] = jnp.where(
+            low, near_ref[0, c : c + 1, :], far_ref[0, c : c + 1, :]
+        )
+
+
+def split_bias(table_ref, count):
+    table = table_ref[:count, :]
+    high = table.astype(jnp.bfloat16)
+    return high, (table - high.astype(jnp.float32)).astype(jnp.bfloat16)
+
+
+def attend_kernel(
+    cont_ref, q_ref, k_ref, v_ref, kp_ref, vp_ref, first_ref, near_ref, far_ref,
+    o_ref, log_ref, table, key_own, key_prev, val_own, val_prev,
 ):
-    key_pos, key_seg, key_index, key_live = geometry
-    bias_high, bias_rest = bias_parts
-    raw = jnp.einsum(
-        "qhd,khd->hqk", query_block, keys_all, preferred_element_type=jnp.float32
-    ) * HEAD ** (-0.5)
-    distance = jnp.maximum(query_pos[:, None] - key_pos[None, :], 0)
-    bucket = jnp.minimum(distance // BUCKET, NB - 1)
-    bucket_hot = (bucket[:, :, None] == jnp.arange(NB, dtype=jnp.int32)[None, None, :]).astype(
-        jnp.bfloat16
-    )
-    raw = raw + jnp.einsum("qkb,hb->hqk", bucket_hot, bias_high, preferred_element_type=jnp.float32)
-    raw = raw + jnp.einsum("qkb,hb->hqk", bucket_hot, bias_rest, preferred_element_type=jnp.float32)
-    allowed = (
-        key_live[None, :]
-        & (key_index[None, :] <= query_index[:, None])
-        & ((key_index[None, :] < tok_len) | (key_seg[None, :] == query_seg[:, None]))
-    )
-    return (jnp.where(allowed[None], raw, NEG), bucket_hot)
+    count = q_ref.shape[1]
+    cont = cont_ref[0] == 1
+    fill_bias(near_ref, far_ref, table)
+    key_own[...] = k_ref[...].T
+    ones = jnp.ones((16, count), jnp.bfloat16)
+    val_own[:HEAD, :] = v_ref[...]
+    val_own[HEAD:, :] = ones
+
+    def finish(o, top, cols):
+        total = o[HEAD : HEAD + 1, :]
+        o_ref[:, cols] = (o[:HEAD, :] / total).astype(jnp.bfloat16)
+        log_ref[0, :, cols] = top + jnp.log(total)
+
+    @pl.when(jnp.logical_not(cont))
+    def _():
+        for b in range(count // SPAN):
+            cols = slice(b * SPAN, (b + 1) * SPAN)
+            keys = (b + 1) * SPAN
+            q = q_ref[:, cols] * jnp.bfloat16(HEAD**-0.5)
+            s = dot(key_own[:keys, :], q) + table[count - b * SPAN : count + SPAN, :]
+            s = jnp.where(iota((keys, SPAN), 0) <= iota((keys, SPAN), 1) + b * SPAN, s, NEG)
+            top = jnp.max(s, axis=0, keepdims=True)
+            p = jnp.exp(s - top).astype(jnp.bfloat16)
+            finish(dot(val_own[:, :keys], p), top, cols)
+
+    @pl.when(cont)
+    def _():
+        high, rest = split_bias(table, count)
+        key_prev[:, :SPAN] = high
+        key_prev[:, SPAN : 2 * SPAN] = rest
+        key_prev[:, 2 * SPAN :] = kp_ref[...].T
+        val_prev[:HEAD, :] = vp_ref[...]
+        val_prev[HEAD:, :] = ones
+        for b in range(count // SPAN):
+            cols = slice(b * SPAN, (b + 1) * SPAN)
+            start = max(b - 1, 0) * SPAN
+            rows = slice(start, (b + 1) * SPAN)
+            keys = (b + 1) * SPAN - start
+            q = q_ref[:, cols] * jnp.bfloat16(HEAD**-0.5)
+            first = first_ref[:, cols]
+            place = iota((1, SPAN), 1) + b * SPAN
+            hot = (iota((SPAN, SPAN), 0) == place - first).astype(jnp.bfloat16)
+            s1 = dot(key_prev[...], jnp.concatenate([hot, hot, q], axis=0))
+            s2 = dot(key_own[rows, :], q) + table[count + start - b * SPAN : count + SPAN, :]
+            at = iota((keys, SPAN), 0) + start
+            s2 = jnp.where((at <= place) & (at >= first), s2, NEG)
+            top = jnp.maximum(
+                jnp.max(s1, axis=0, keepdims=True), jnp.max(s2, axis=0, keepdims=True)
+            )
+            p1 = jnp.exp(s1 - top).astype(jnp.bfloat16)
+            p2 = jnp.exp(s2 - top).astype(jnp.bfloat16)
+            finish(dot(val_prev[...], p1) + dot(val_own[:, rows], p2), top, cols)
+
+
+def attend(cont, proj, prev, first, near, far):
+    heads, count = proj.shape[0] // (3 * HEAD), proj.shape[1]
+    part = lambda k: pl.BlockSpec((HEAD, count), lambda h: (h + k * heads, 0))
+    table = pl.BlockSpec((1,) + near.shape[1:], lambda h: (h, 0, 0))
+    return pl.pallas_call(
+        attend_kernel,
+        grid=(heads,),
+        in_specs=[
+            pl.BlockSpec(memory_space=pltpu.SMEM),
+            part(0), part(1), part(2), part(0), part(1),
+            pl.BlockSpec((1, count), lambda h: (0, 0)),
+            table, table,
+        ],
+        out_specs=[part(0), pl.BlockSpec((1, 1, count), lambda h: (h, 0, 0))],
+        out_shape=[
+            jax.ShapeDtypeStruct((heads * HEAD, count), jnp.bfloat16),
+            jax.ShapeDtypeStruct((heads, 1, count), jnp.float32),
+        ],
+        scratch_shapes=[
+            pltpu.VMEM((2 * count, SPAN), jnp.float32),
+            pltpu.VMEM((count, HEAD), jnp.bfloat16),
+            pltpu.VMEM((count, HEAD + 2 * SPAN), jnp.bfloat16),
+            pltpu.VMEM((HEAD + 16, count), jnp.bfloat16),
+            pltpu.VMEM((HEAD + 16, count), jnp.bfloat16),
+        ],
+        compiler_params=WIDE,
+        name="attend",
+    )(cont, proj, proj, proj, prev, prev, first, near, far)
+
+
+def attend_back_kernel(
+    cont_ref, q_ref, k_ref, v_ref, kp_ref, vp_ref, first_ref, near_ref, far_ref, o_ref, log_ref, do_ref,
+    dq_ref, dk_ref, dv_ref, dkp_ref, dvp_ref, sum_near_ref, sum_far_ref,
+    table, key_own, key_prev, val_own, val_prev, q_cat, q_nat, do_nat, hot_nat, dtable, dq, dk, dv,
+):
+    count = q_ref.shape[1]
+    blocks = count // SPAN
+    cont = cont_ref[0] == 1
+    fill_bias(near_ref, far_ref, table)
+    key_own[...] = k_ref[...].T
+    val_own[...] = v_ref[...].T
+    q = q_ref[...] * jnp.bfloat16(HEAD**-0.5)
+    q_cat[2 * SPAN :, :] = q
+    q_nat[...] = q.T
+    do_nat[...] = do_ref[...].T
+    dtable[...] = jnp.zeros_like(dtable)
+    dq[...] = jnp.zeros_like(dq)
+    dk[...] = jnp.zeros_like(dk)
+    dv[...] = jnp.zeros_like(dv)
+    delta = jnp.sum(
+        do_ref[...].astype(jnp.float32) * o_ref[...].astype(jnp.float32), axis=0, keepdims=True
+    )
+
+    def tile(kb, qb):
+        rows = slice(kb * SPAN, (kb + 1) * SPAN)
+        cols = slice(qb * SPAN, (qb + 1) * SPAN)
+        where = slice(count + (kb - qb) * SPAN, count + (kb - qb + 1) * SPAN)
+        s = dot(key_own[rows, :], q_cat[2 * SPAN :, cols]) + table[where, :]
+        at = iota((SPAN, SPAN), 0) + kb * SPAN
+        live = (at <= iota((SPAN, SPAN), 1) + qb * SPAN) & (at >= first_ref[:, cols])
+        p = jnp.exp(jnp.where(live, s, NEG) - log_ref[0, :, cols])
+        dp = dot(val_own[rows, :], do_ref[:, cols])
+        ds = p * (dp - delta[:, cols])
+        dtable[where, :] += ds
+        ds = ds.astype(jnp.bfloat16)
+        dk[rows, :] += dot(ds, q_nat[cols, :])
+        dv[rows, :] += dot(p.astype(jnp.bfloat16), do_nat[cols, :])
+        dq[:, cols] += dot(k_ref[:, rows], ds)
+
+    for kb in range(blocks):
+        for qb in range(kb, min(kb + 2, blocks)):
+            tile(kb, qb)
+
+    @pl.when(jnp.logical_not(cont))
+    def _():
+        for kb in range(blocks):
+            for qb in range(kb + 2, blocks):
+                tile(kb, qb)
+
+    @pl.when(cont)
+    def _():
+        high, rest = split_bias(table, count)
+        key_prev[:, :SPAN] = high
+        key_prev[:, SPAN : 2 * SPAN] = rest
+        key_prev[:, 2 * SPAN :] = kp_ref[...].T
+        val_prev[...] = vp_ref[...].T
+        hot = (iota((SPAN, count), 0) == iota((1, count), 1) - first_ref[...]).astype(jnp.bfloat16)
+        q_cat[:SPAN, :] = hot
+        q_cat[SPAN : 2 * SPAN, :] = hot
+        hot_nat[...] = hot.T
+
+        for kb in range(blocks):
+            rows = slice(kb * SPAN, (kb + 1) * SPAN)
+            s = dot(key_prev[rows, :], q_cat[...])
+            p = jnp.exp(s - log_ref[0])
+            dp = dot(val_prev[rows, :], do_ref[...])
+            ds = (p * (dp - delta)).astype(jnp.bfloat16)
+            dkp_ref[:, rows] = dot(ds, q_nat[...]).astype(jnp.bfloat16).T
+            dvp_ref[:, rows] = dot(p.astype(jnp.bfloat16), do_nat[...]).astype(jnp.bfloat16).T
+            dtable[rows, :] += dot(ds, hot_nat[...])
+            dq[...] += dot(kp_ref[:, rows], ds)
+
+    dq_ref[...] = (dq[...] * HEAD**-0.5).astype(jnp.bfloat16)
+    dk_ref[...] = dk[...].astype(jnp.bfloat16).T
+    dv_ref[...] = dv[...].astype(jnp.bfloat16).T
+    low = (iota((BUCKET, SPAN), 1) & (BUCKET - 1)) >= iota((BUCKET, SPAN), 0)
+    for c in range(2 * count // BUCKET):
+        part = dtable[c * BUCKET : (c + 1) * BUCKET, :]
+        near = jnp.sum(jnp.where(low, part, 0.0), axis=0, keepdims=True)
+        sum_near_ref[0, c : c + 1, :] = near
+        sum_far_ref[0, c : c + 1, :] = jnp.sum(part, axis=0, keepdims=True) - near
+
+
+def attend_back(cont, proj, prev, first, near, far, o, log, do):
+    heads, count = proj.shape[0] // (3 * HEAD), proj.shape[1]
+    part = lambda k: pl.BlockSpec((HEAD, count), lambda h: (h + k * heads, 0))
+    table = pl.BlockSpec((1,) + near.shape[1:], lambda h: (h, 0, 0))
+    grad = jax.ShapeDtypeStruct((heads * HEAD, count), jnp.bfloat16)
+    sums = jax.ShapeDtypeStruct(near.shape, jnp.float32)
+    return pl.pallas_call(
+        attend_back_kernel,
+        grid=(heads,),
+        in_specs=[
+            pl.BlockSpec(memory_space=pltpu.SMEM),
+            part(0), part(1), part(2), part(0), part(1),
+            pl.BlockSpec((1, count), lambda h: (0, 0)),
+            table, table, part(0),
+            pl.BlockSpec((1, 1, count), lambda h: (h, 0, 0)),
+            part(0),
+        ],
+        out_specs=[part(0)] * 5 + [table] * 2,
+        out_shape=[grad] * 5 + [sums] * 2,
+        scratch_shapes=[
+            pltpu.VMEM((2 * count, SPAN), jnp.float32),
+            pltpu.VMEM((count, HEAD), jnp.bfloat16),
+            pltpu.VMEM((count, HEAD + 2 * SPAN), jnp.bfloat16),
+            pltpu.VMEM((count, HEAD), jnp.bfloat16),
+            pltpu.VMEM((count, HEAD), jnp.bfloat16),
+            pltpu.VMEM((HEAD + 2 * SPAN, count), jnp.bfloat16),
+            pltpu.VMEM((count, HEAD), jnp.bfloat16),
+            pltpu.VMEM((count, HEAD), jnp.bfloat16),
+            pltpu.VMEM((count, SPAN), jnp.bfloat16),
+            pltpu.VMEM((2 * count, SPAN), jnp.float32),
+            pltpu.VMEM((HEAD, count), jnp.float32),
+            pltpu.VMEM((count, HEAD), jnp.float32),
+            pltpu.VMEM((count, HEAD), jnp.float32),
+        ],
+        compiler_params=WIDE,
+        name="attend_back",
+    )(cont, proj, proj, proj, prev, prev, first, near, far, o, log, do)
+
+
+def bias_levels(bias, count):
+    rows, lanes = 2 * count // BUCKET, SPAN // BUCKET
+    step = jnp.arange(lanes)[None, :] - jnp.arange(rows)[:, None] + rows // 2
+    names = jnp.arange(NB)
+    near_hot = (jnp.clip(step, 0, NB - 1)[..., None] == names).astype(jnp.float32)
+    far_hot = (jnp.clip(step - 1, 0, NB - 1)[..., None] == names).astype(jnp.float32)
+    return near_hot, far_hot
+
+
+def bias_tables(bias, count):
+    out = []
+    for hot in bias_levels(bias, count):
+        level = jnp.sum(hot[None] * bias[:, None, None, :], axis=-1)
+        out.append(jnp.repeat(level, BUCKET, axis=2))
+    return out
+
+
+def bias_totals(sum_near, sum_far, count):
+    total = 0.0
+    for hot, sums in zip(bias_levels(None, count), (sum_near, sum_far)):
+        level = jnp.sum(sums.reshape(sums.shape[0], sums.shape[1], -1, BUCKET), axis=-1)
+        total = total + jnp.sum(level[..., None] * hot[None], axis=(1, 2))
+    return total
 
 
 def root_mean_square_pullback(normalized_gradient, local_gain, unit_scaled_input, inverse_norm):
@@ -130,8 +362,6 @@
     cap_rows = 2 * tok_len // experts
     inner_local = w_qkv.shape[2]
     heads_local = inner_local // HEAD
-    block_rows = min(512, tok_len)
-    block_count = tok_len // block_rows
     qkv_full, proj_full, win_full, wout_full = (
         lax.all_gather(w_qkv, "my", axis=0, tiled=True),
         lax.all_gather(w_out_attn, "my", axis=1, tiled=True),
@@ -142,41 +372,20 @@
     x_full = feature_gather(block_entry_rows).astype(jnp.float32)
     first_inverse_norm = lax.rsqrt(jnp.mean(x_full * x_full, axis=1, keepdims=True) + EPS)
     normed_one = (x_full * first_inverse_norm * gain_one).astype(jnp.bfloat16)
-    projected = jnp.dot(normed_one, qkv_flat, preferred_element_type=jnp.float32).astype(
-        jnp.bfloat16
-    )
-    queries = projected[:, :inner_local].reshape(tok_len, heads_local, HEAD)
-    keys_own = projected[:, inner_local : 2 * inner_local].reshape(tok_len, heads_local, HEAD)
-    vals_own = projected[:, 2 * inner_local :].reshape(tok_len, heads_local, HEAD)
-    keys_prev, vals_prev = from_behind((keys_own, vals_own), "my", 1)
-    keys_all = jnp.concatenate([keys_prev, keys_own], axis=0)
-    vals_all = jnp.concatenate([vals_prev, vals_own], axis=0)
-    own_pos, own_seg, own_index, geometry = layout(cont_ids[0], is_cont, tok_len)
+    projected = lax.dot_general(
+        qkv_flat, normed_one, (((0,), (1,)), ((), ())), preferred_element_type=jnp.float32
+    ).astype(jnp.bfloat16)
+    earlier = from_behind(projected[inner_local:], "my", 1)
+    index = jnp.arange(tok_len, dtype=jnp.int32)
+    same_seg = cont_ids[0][:, None] == cont_ids[0][None, :]
+    first_pos = jnp.min(jnp.where(same_seg, index[:, None], tok_len), axis=0, keepdims=True)
+    first_pos = jnp.where(is_cont, first_pos, 0)
     bias_local = lax.dynamic_slice_in_dim(rel_bias, feat_index * heads_local, heads_local, 0)
-    bias_high = bias_local.astype(jnp.bfloat16)
-    bias_rest = (bias_local - bias_high.astype(jnp.float32)).astype(jnp.bfloat16)
-    bias_parts = (bias_high, bias_rest)
-    query_blocks = queries.reshape(block_count, block_rows, heads_local, HEAD)
-    pos_blocks = own_pos.reshape(block_count, block_rows)
-    seg_blocks = own_seg.reshape(block_count, block_rows)
-    index_blocks = own_index.reshape(block_count, block_rows)
-
-    def forward_block(packed):
-        query_block, query_pos, query_seg, query_index = packed
-        scores, bucket_hot = block_scores(
-            query_block, keys_all, bias_parts, query_pos, query_seg, query_index, geometry, tok_len
-        )
-        row_top = jnp.max(scores, axis=-1, keepdims=True)
-        exp_terms = jnp.exp(scores - row_top)
-        row_sum = jnp.sum(exp_terms, axis=-1, keepdims=True)
-        probs = (exp_terms / row_sum).astype(jnp.bfloat16)
-        block_out = jnp.einsum("hqk,khd->qhd", probs, vals_all, preferred_element_type=jnp.float32)
-        return (block_out.astype(jnp.bfloat16), (row_top + jnp.log(row_sum))[..., 0])
-
-    mixed_blocks, log_sums = lax.map(
-        forward_block, (query_blocks, pos_blocks, seg_blocks, index_blocks)
-    )
-    mixed = mixed_blocks.reshape(tok_len, inner_local)
+    near, far = bias_tables(bias_local, tok_len)
+    cont_flag = is_cont.astype(jnp.int32).reshape(1)
+    geometry = (cont_flag, projected, earlier, first_pos, near, far)
+    mixed_rows, log_sums = attend(*geometry)
+    mixed = mixed_rows.T
     branch = feature_sum(jnp.dot(mixed, proj_full, preferred_element_type=jnp.float32))
     hidden_activation = block_entry_rows.astype(jnp.float32) + branch
     second_inverse_norm = lax.rsqrt(
@@ -266,58 +475,16 @@
     grad_proj = lax.dot_general(
         mixed, hidden_full, (((0,), (0,)), ((), ())), preferred_element_type=jnp.float32
     )
-    grad_blocks = mixed_grad.reshape(block_count, block_rows, heads_local, HEAD)
-
-    def backward_block(carry, packed):
-        keys_grad, vals_grad, bias_grad = carry
-        query_block, query_pos, query_seg, query_index, out_grad, log_sum = packed
-        scores, bucket_hot = block_scores(
-            query_block, keys_all, bias_parts, query_pos, query_seg, query_index, geometry, tok_len
-        )
-        probs = jnp.exp(scores - log_sum[..., None])
-        prob_grad = jnp.einsum(
-            "qhd,khd->hqk", out_grad, vals_all, preferred_element_type=jnp.float32
-        )
-        row_delta = jnp.sum(probs * prob_grad, axis=-1, keepdims=True)
-        score_grad = (probs * (prob_grad - row_delta)).astype(jnp.bfloat16)
-        query_grad = jnp.einsum(
-            "hqk,khd->qhd", score_grad, keys_all, preferred_element_type=jnp.float32
-        ) * HEAD ** (-0.5)
-        keys_grad = keys_grad + jnp.einsum(
-            "hqk,qhd->khd", score_grad, query_block, preferred_element_type=jnp.float32
-        ) * HEAD ** (-0.5)
-        vals_grad = vals_grad + jnp.einsum(
-            "hqk,qhd->khd", probs.astype(jnp.bfloat16), out_grad, preferred_element_type=jnp.float32
-        )
-        bucket_sums = jnp.einsum(
-            "hqk,qkb->hb", score_grad, bucket_hot, preferred_element_type=jnp.float32
-        )
-        return ((keys_grad, vals_grad, bias_grad + bucket_sums), query_grad)
-
-    start_carry = (
-        jnp.zeros((2 * tok_len, heads_local, HEAD), jnp.float32),
-        jnp.zeros((2 * tok_len, heads_local, HEAD), jnp.float32),
-        jnp.zeros((heads_local, NB), jnp.float32),
-    )
-    (keys_grad, vals_grad, bias_grad), query_grads = lax.scan(
-        backward_block,
-        start_carry,
-        (query_blocks, pos_blocks, seg_blocks, index_blocks, grad_blocks, log_sums),
-    )
-    keys_back, vals_back = (
-        from_behind(keys_grad[:tok_len].astype(jnp.bfloat16), "my", -1).astype(jnp.float32),
-        from_behind(vals_grad[:tok_len].astype(jnp.bfloat16), "my", -1).astype(jnp.float32),
-    )
-    own_keys_grad = keys_grad[tok_len:] + keys_back
-    own_vals_grad = vals_grad[tok_len:] + vals_back
-    proj_grad = jnp.concatenate(
-        [
-            query_grads.reshape(tok_len, inner_local),
-            own_keys_grad.reshape(tok_len, inner_local),
-            own_vals_grad.reshape(tok_len, inner_local),
-        ],
-        axis=1,
+    (
+        query_grad, keys_grad, vals_grad, keys_back, vals_back, near_sums, far_sums
+    ) = attend_back(*geometry, mixed_rows, log_sums, mixed_grad.T)
+    bias_grad = bias_totals(near_sums, far_sums, tok_len)
+    returned_grad = from_behind(jnp.concatenate([keys_back, vals_back], axis=0), "my", -1)
+    own_grad = (
+        jnp.concatenate([keys_grad, vals_grad], axis=0).astype(jnp.float32)
+        + returned_grad.astype(jnp.float32)
     ).astype(jnp.bfloat16)
+    proj_grad = jnp.concatenate([query_grad, own_grad], axis=0).T
     grad_qkv = lax.dot_general(
         normed_one, proj_grad, (((0,), (0,)), ((), ())), preferred_element_type=jnp.float32
     ).reshape(qkv_full.shape[0], 3, inner_local)

time: 1490 us -> 857 us (0.58)
  matrix products: 417 us -> 58.2 us
  local copies, waits for them, and re-layouts: 279 us -> 158 us
  waiting for transfers between devices: 543 us -> 431 us
  other arithmetic: 91 us -> 46.5 us
  Pallas kernels: 0 us -> 17.3 us
    dot_general x25 -> x1, matrix products: 357 us -> 2.59 us  [body(): lax.dot_general(qkv_flat, normed_one, (((0,), (1,)), ((), ())), preferred...]
    unnamed x21, waiting for transfers between devices: 193 us -> 106 us
    dot_general x4 -> x0, local copies, waits for them, and re-layouts: 69.7 us -> none  [the longest x2 34.9 us: block_scores(): jnp.einsum('qkb,hb->hqk', bucket_hot, bias_high, preferred_element_type=j...]
    reduce_scatter x2, waiting for transfers between devices: 118 us -> 78.1 us  [feature_sum(): lax.psum_scatter(values.astype(jnp.bfloat16), 'mx', scatter_dimension=1,...]
    convert_element_type x2, local copies, waits for them, and re-layouts: 28.3 us -> 3.8 us  [feature_sum(): values.astype(jnp.bfloat16)]
    convert_element_type x3, other arithmetic: 18.9 us -> 1.45 us  [the longest x1 1.43 us: body(): own_grad = (jnp.concatenate([keys_grad, vals_grad], axis=0).astype(jnp.fl...]
    pallas_call x0 -> x2, Pallas kernels: none -> 17.3 us  [the longest x1 11.9 us: attend_back(): pl.pallas_call(attend_back_kernel, grid=(heads,), in_specs=[pl.BlockSpec(...]
    while x50 -> x0, local copies, waits for them, and re-layouts: 15 us -> none
  transfers between devices with their start and end apart: 22 -> 20, of which waited for: 12 -> 13; matrix products, arithmetic and copies ran while one was open for 14% -> 21% of each run, Pallas kernels for 0% -> 0%
where the time goes in v1:
time: 857 us; the launch traced here: 847 us
  waiting for transfers between devices  431 us (50%)
  local copies, waits for them, and re-layouts  158 us (18%)
  blocking collectives  107 us (12%)
  matrix products  58.2 us (7%)
  other arithmetic  46.5 us (5%)
  Pallas kernels  17.3 us (2%)
  between operations  15.3 us (2%)
  starting transfers between devices  13 us (2%)
    all_gather x5, waiting for transfers between devices, feature_gather(): return lax.all_gather(values, 'mx', axis=1, tiled=True)  181 us
    unnamed x21, waiting for transfers between devices  106 us
    reduce_scatter x2, waiting for transfers between devices, feature_sum(): lax.psum_scatter(values.astype(jnp.bfloat16), 'mx', scatter_dimension=1,...  78.1 us
    psum x1, waiting for transfers between devices, body(): lax.psum(grad_qkv.astype(jnp.bfloat16), 'dp').astype(jnp.float32)  42.5 us
    psum x1, blocking collectives, body(): lax.psum((full_bias, full_gain_one, full_gain_two, full_router), ('dp', '...  40.3 us
    psum x4, blocking collectives, row_dot_total(): return lax.psum(values, 'mx')  38.5 us
    unnamed x73, local copies, waits for them, and re-layouts  38.3 us
    all_to_all x2, blocking collectives, expert_swap(): return lax.all_to_all(values, 'dp', split_axis=0, concat_axis=0, tiled=True)  23.8 us
  transfers between devices with their start and end apart: 20, of which 13 were waited for; matrix products, arithmetic and copies ran while one was open for 21% of the time, Pallas kernels for 0%

profile of v1, /device:TPU:0, one launch (start us, length us, event | category | flops | bytes accessed | tf_op | source)
XLA Modules:
  0.0 847.2 jit_solution(4708136047319536949)
XLA Ops:
  11.6 37.8 %all-gather.8.cloned.1.call-done = bf16[1024,768]{0,1:T(8,128)(2,1)} async-done(((bf16[1024,192]{0,1:T(8,128)(2,1)}), bf16[1024,768]{0,1:T(8,128)(2,1)}) %all-gather.8.cloned.1.call-update) | async-done | bytes 1572880 | tf_op jit(solution)/shard_map/all_gather | solution.py:25
  68.1 44.1 %reduce-scatter.19.cloned.1.call-done = bf16[1024,192]{0,1:T(8,128)(2,1)} async-done(((bf16[1024,768]{0,1:T(8,128)(2,1)}), bf16[1024,192]{0,1:T(8,128)(2,1)}) %reduce-scatter.19.cloned.1.call-update) | async-done | bytes 393232 | tf_op jit(solution)/shard_map/reduce_scatter | solution.py:29
  113.4 9.8 %psum.70 = f32[1024,1]{0,1:T(1,128)S(1)} all-reduce(f32[1024,1]{0,1:T(1,128)S(1)} %bitcast.192), channel_id=1, replica_groups=mesh['dp'=4,'mx'=4,'my'=2] {'mx'}, use_global_device_ids=true, to_apply=%region_6.7 | all-reduce | flops 1024 | bytes 8192 | tf_op jit(solution)/shard_map/psum | solution.py:35
  125.7 11.8 %gather_fusion = s32[2048]{0:T(1024)S(1)} fusion(s32[2048]{0:T(1024)S(1)} %reshape.284, s32[2048]{0:T(1024)S(1)} %broadcast_clamp_fusion.2), kind=kCustom, calls=%fused_computation.2 | custom fusion | bytes 24576 | tf_op jit(solution)/shard_map/gather | solution.py:44
  171.0 9.1 %gather_fusion.1 = bf16[2048,192]{1,0:T(8,128)(2,1)} fusion(bf16[1024,192]{1,0:T(8,128)(2,1)S(1)} %copy.146, s32[2048]{0:T(1024)S(1)} %get-tuple-element.50), kind=kCustom, calls=%fused_computation.3 | custom fusion | bytes 1581056 | tf_op jit(solution)/shard_map/jit(_take)/gather | solution.py:408
  187.3 9.1 %gather_fusion.2 = bf16[2048,192]{1,0:T(8,128)(2,1)} fusion(bf16[2048,192]{1,0:T(8,128)(2,1)S(1)} %multiply_convert_fusion, s32[2048]{0:T(1024)S(1)} %get-tuple-element.49), kind=kCustom, calls=%fused_computation.4 | custom fusion | bytes 1581056 | tf_op jit(solution)/shard_map/jit(_take)/gather | solution.py:433
  200.1 12.9 %all_to_all.20 = bf16[4,512,192]{1,2,0:T(8,128)(2,1)S(1)} all-to-all(bf16[4,512,192]{1,2,0:T(8,128)(2,1)S(1)} %get-tuple-element.51), channel_id=1, replica_groups=mesh['dp'=4,'mx'=4,'my'=2] {'dp'}, dimensions={0} | all-to-all | bytes 1572864 | tf_op jit(solution)/shard_map/all_to_all | solution.py:39
  214.0 10.9 %all_to_all.21 = bf16[4,512,192]{1,2,0:T(8,128)(2,1)S(1)} all-to-all(bf16[4,512,192]{1,2,0:T(8,128)(2,1)S(1)} %copy-done.15), channel_id=1, replica_groups=mesh['dp'=4,'mx'=4,'my'=2] {'dp'}, dimensions={0} | all-to-all | bytes 1572864 | tf_op jit(solution)/shard_map/all_to_all | solution.py:39
  227.7 46.7 %all-gather.18.cloned.1.call-done = bf16[2048,768]{0,1:T(8,128)(2,1)} async-done(((bf16[2048,192]{0,1:T(8,128)(2,1)}), bf16[2048,768]{0,1:T(8,128)(2,1)}) %all-gather.18.cloned.1.call-update) | async-done | bytes 3145744 | tf_op jit(solution)/shard_map/all_gather | solution.py:25
  279.1 59.5 %all-gather.12.cloned.1.call-done = bf16[2048,768]{0,1:T(8,128)(2,1)} async-done(((bf16[2048,192]{0,1:T(8,128)(2,1)}), bf16[2048,768]{0,1:T(8,128)(2,1)}) %all-gather.12.cloned.1.call-update) | async-done | bytes 3145744 | tf_op jit(solution)/shard_map/all_gather | solution.py:25
  395.1 48.4 %reduce-scatter.27.cloned.1.call-done = bf16[192,2048]{1,0:T(8,128)(2,1)} async-done(((bf16[768,2048]{1,0:T(8,128)(2,1)}), bf16[192,2048]{1,0:T(8,128)(2,1)}) %reduce-scatter.27.cloned.1.call-update) | async-done | bytes 786448
  450.8 55.3 %reduce-scatter.25.cloned.1.call-done = bf16[192,2048]{1,0:T(8,128)(2,1)} async-done(((bf16[768,2048]{1,0:T(8,128)(2,1)}), bf16[192,2048]{1,0:T(8,128)(2,1)}) %reduce-scatter.25.cloned.1.call-update) | async-done | bytes 786448
  518.2 9.1 %gather_fusion.4 = bf16[2048,192]{1,0:T(8,128)(2,1)} fusion(bf16[2048,192]{1,0:T(8,128)(2,1)S(1)} %bitcast.150, s32[2048]{0:T(1024)S(1)} %broadcast_clamp_fusion.1), kind=kCustom, calls=%fused_computation.1.clone | custom fusion | bytes 1581056 | tf_op jit(solution)/shard_map/jit(_take)/gather | solution.py:453
  531.0 9.1 %gather_fusion.3 = bf16[2048,192]{1,0:T(8,128)(2,1)} fusion(bf16[2048,192]{1,0:T(8,128)(2,1)S(1)} %bitcast.149, s32[2048]{0:T(1024)S(1)} %broadcast_clamp_fusion.1), kind=kCustom, calls=%fused_computation.clone | custom fusion | bytes 1581056 | tf_op jit(solution)/shard_map/jit(_take)/gather | solution.py:424
  542.5 15.8 %multiply_reduce_fusion = (f32[1024,2]{1,0:T(8,128)S(1)}, f32[1024,192]{1,0:T(8,128)}, f32[1024,192]{1,0:T(8,128)}) fusion(f32[1024,192]{1,0:T(8,128)S(1)} %copy.156, f32[1024,2]{1,0:T(8,128)} %reshape.299, bf16[1024,2,192]{2,1,0:T(2,128)(2,1)} %reshape.375, pred[1024,2]{1,0:T(8,128)(4,1)S(1)} %compare_and_fusion, f32[1024,2]{1,0:T(8,128)} %copy-done.10, ...), kind=kLoop, calls=%fused_computation.51 | loop fusion | flops 3930112 | bytes 3958784 | tf_op jit(solution)/shard_map/reduce_sum | solution.py:427
  558.4 10.6 %psum.71 = f32[1024,2]{0,1:T(2,128)S(1)} all-reduce(f32[1024,2]{0,1:T(2,128)S(1)} %copy.164), channel_id=1, replica_groups=mesh['dp'=4,'mx'=4,'my'=2] {'mx'}, use_global_device_ids=true, to_apply=%region_21.23 | all-reduce | flops 2048 | bytes 16384 | tf_op jit(solution)/shard_map/psum | solution.py:35
  582.9 37.2 %all-gather.20.cloned.1.call-done = bf16[1024,768]{0,1:T(8,128)(2,1)} async-done(((bf16[1024,192]{0,1:T(8,128)(2,1)}), bf16[1024,768]{0,1:T(8,128)(2,1)}) %all-gather.20.cloned.1.call-update) | async-done | bytes 1572880 | tf_op jit(solution)/shard_map/all_gather | solution.py:25
  622.0 11.9 %attend_back.1 = (bf16[192,1024]{1,0:T(8,128)(2,1)S(1)}, bf16[192,1024]{1,0:T(8,128)(2,1)S(1)}, bf16[192,1024]{1,0:T(8,128)(2,1)S(1)}, bf16[192,1024]{1,0:T(8,12...) custom-call(s32[1]{0:T(128)} %bitcast.cont_ref, ...), custom_call_target="tpu_custom_call" | custom-call | tf_op jit(solution)/shard_map/attend_back/pallas_call | solution.py:268
  637.9 11.0 %collective-permute-done.1 = bf16[384,1024]{1,0:T(8,128)(2,1)} collective-permute-done((bf16[384,1024]{1,0:T(8,128)(2,1)}, bf16[384,1024]{1,0:T(8,128)(2,1)}, u32[]{:S(2)}, u32[]{:S(2)}) %collective-permute-start.1) | collective-permute-done | bytes 786464 | tf_op jit(solution)/shard_map/ppermute | solution.py:21
  654.6 9.2 %bitcast_convert_fusion = bf16[2,768,768]{2,1,0:T(8,128)(2,1)} fusion(bf16[4,2,256,768]{3,2,1,0:T(8,128)(2,1)} %bitcast.165, f32[2,4,256,768]{3,2,1,0:T(8,128)} %fusion.20), kind=kOutput, calls=%fused_computation.28 | convolution fusion | flops 2431254528 | bytes 11796480 | tf_op jit(solution)/shard_map/sjcf,sjcd->jfd/dot_general | solution.py:441
  705.8 42.5 %all-reduce.4.cloned.1.call-done = (bf16[384,3,192]{0,2,1:T(8,128)(2,1)}, bf16[192,384]{1,0:T(8,128)(2,1)}) async-done(((bf16[384,3,192]{0,2,1:T(8,128)(2,1)}, bf16[192,384]{1,0:T(8,128)(2,1)}), (bf16[384,3,192]{0,2,1:T(8,128)(2,1)}, bf16[192,384]{1,0:T(8,128)(2,1)})) %all-reduce.4.cloned.1.call-update) | async-done | bytes 589840 | tf_op jit(solution)/shard_map/psum | solution.py:517
  752.0 34.0 %reduce-scatter.21.cloned.1.call-done = bf16[1024,192]{0,1:T(8,128)(2,1)} async-done(((bf16[1024,768]{0,1:T(8,128)(2,1)}), bf16[1024,192]{0,1:T(8,128)(2,1)}) %reduce-scatter.21.cloned.1.call-update) | async-done | bytes 393232 | tf_op jit(solution)/shard_map/reduce_scatter | solution.py:29
  787.2 9.8 %psum.73 = f32[1024,1]{0,1:T(1,128)S(1)} all-reduce(f32[1024,1]{0,1:T(1,128)S(1)} %bitcast.191), channel_id=1, replica_groups=mesh['dp'=4,'mx'=4,'my'=2] {'mx'}, use_global_device_ids=true, to_apply=%region_28.30 | all-reduce | flops 1024 | bytes 8192 | tf_op jit(solution)/shard_map/psum | solution.py:35
  797.2 40.3 %all-reduce = (f32[12,32]{1,0:T(8,128)}, f32[768]{0:T(1024)}, f32[768]{0:T(1024)}, f32[768,8]{0,1:T(8,128)}) all-reduce(f32[12,32]{1,0:T(8,128)S(1)} %dynamic_update_slice.12, f32[768]{0:T(1024)S(1)} %dynamic_update_slice.13, f32[768]{0:T(1024)S(1)} %dynamic_update_slice.14, ...), channel_id=1, replica_groups=mesh['dp'=4,'mx'=4,'my'=2] {'dp','mx','my'}, use_global_device_ids=true, to_apply=%region_37.39 | all-reduce | flops 8064 | bytes 64512 | tf_op jit(solution)/shard_map/psum | solution.py:532
  (240 shorter events, 236.2 us)
Async XLA Ops:
  7.2 175.1 %copy-start = (bf16[768,8]{0,1:T(8,128)(2,1)S(1)}, bf16[768,8]{0,1:T(8,128)(2,1)}, u32[]{:S(2)}) copy-start(bf16[768,8]{0,1:T(8,128)(2,1)} %param.22) | copy-start | bytes 36868
  7.2 42.2 %all-gather.8.cloned.1.call-start = ((), (), s32[]{:S(2)}) async-start(), calls=%async_computation.12 | async-start | bytes 1966080 | tf_op jit(solution)/shard_map/all_gather | solution.py:25
  7.9 104.2 %reduce-scatter.19.cloned.1.call-start = ((), (), s32[]{:S(2)}) async-start(), calls=%async_computation.13 | async-start | bytes 1966080 | tf_op jit(solution)/shard_map/reduce_scatter | solution.py:29
  54.8 5.2 collective-permute-start
  67.2 115.0 %all-gather.10.cloned.1.call-start = ((), (), s32[]{:S(2)}) async-start(), calls=%async_computation.14 | async-start | bytes 1966080 | tf_op jit(solution)/shard_map/all_gather | solution.py:25
  125.1 149.4 %all-gather.18.cloned.1.call-start = ((), (), s32[]{:S(2)}) async-start(), calls=%async_computation.18 | async-start | bytes 3932160 | tf_op jit(solution)/shard_map/all_gather | solution.py:25
  214.0 124.6 %all-gather.12.cloned.1.call-start = ((), (), s32[]{:S(2)}) async-start(), calls=%async_computation.15 | async-start | bytes 3932160 | tf_op jit(solution)/shard_map/all_gather | solution.py:25
  226.0 123.7 %all-gather.14.cloned.1.call-start = ((), (), s32[]{:S(2)}) async-start(), calls=%async_computation.16 | async-start | bytes 3538944 | tf_op jit(solution)/shard_map/all_gather | solution.py:368
  226.5 136.7 %all-gather.16.cloned.1.call-start = ((), (), s32[]{:S(2)}) async-start(), calls=%async_computation.17 | async-start | bytes 3538944 | tf_op jit(solution)/shard_map/all_gather | solution.py:369
  227.3 216.2 %reduce-scatter.27.cloned.1.call-start = ((), (), s32[]{:S(2)}) async-start(), calls=%async_computation.23 | async-start | bytes 3932160
  381.9 124.2 %reduce-scatter.25.cloned.1.call-start = ((), (), s32[]{:S(2)}) async-start(), calls=%async_computation.22 | async-start | bytes 3932160
  446.2 64.4 %all-to-all-start.3 = ((bf16[4,512,192]{1,2,0:T(8,128)(2,1)}), bf16[4,512,192]{1,2,0:T(8,128)(2,1)}, u32[]{:S(2)}, u32[]{:S(2)}) async-start(bf16[4,512,192]{1,2,0:T(8,128)(2,1)} %copy.162), calls=%async_computation.4 | async-start | bytes 1572864 | tf_op jit(solution)/shard_map/all_to_all | solution.py:39
  510.5 19.1 %all-to-all-start.1 = ((bf16[4,512,192]{1,2,0:T(8,128)(2,1)}), bf16[4,512,192]{1,2,0:T(8,128)(2,1)}, u32[]{:S(2)}, u32[]{:S(2)}) async-start(bf16[4,512,192]{1,2,0:T(8,128)(2,1)} %copy.152), calls=%async_computation.2 | async-start | bytes 1572864 | tf_op jit(solution)/shard_map/all_to_all | solution.py:39
  514.7 105.4 %all-gather.20.cloned.1.call-start = ((), (), s32[]{:S(2)}) async-start(), calls=%async_computation.19 | async-start | bytes 1966080 | tf_op jit(solution)/shard_map/all_gather | solution.py:25
  582.8 98.4 %reduce-scatter.31.cloned.1.call-start = ((), (), s32[]{:S(2)}) async-start(), calls=%async_computation.25 | async-start | bytes 589824
  634.9 14.0 %collective-permute-start.1 = (bf16[384,1024]{1,0:T(8,128)(2,1)}, bf16[384,1024]{1,0:T(8,128)(2,1)}, u32[]{:S(2)}, u32[]{:S(2)}) collective-permute-start(bf16[384,1024]{1,0:T(8,128)(2,1)} %pad_maximum_fusion.1), channel_id=1, source_target_pairs={{1,0},{3,2},{5,4},{7,6},{9,8},{11,10},{13,12},{15,14},{17,16},{19,... | collective-permute-start | bytes 2359304 | tf_op jit(solution)/shard_map/ppermute | solution.py:21
  637.8 45.2 %reduce-scatter.29.cloned.1.call-start = ((), (), s32[]{:S(2)}) async-start(), calls=%async_computation.24 | async-start | bytes 1474560
  654.3 33.8 %reduce-scatter.33.cloned.1.call-start = ((), (), s32[]{:S(2)}) async-start(), calls=%async_computation.26 | async-start | bytes 3538944
  674.1 23.4 %reduce-scatter.23.cloned.1.call-start = ((), (), s32[]{:S(2)}) async-start(), calls=%async_computation.21 | async-start | bytes 3538944 | tf_op jit(solution)/shard_map/reduce_scatter | solution.py:509
  681.2 67.2 %all-reduce.4.cloned.1.call-start = ((), (), s32[]{:S(2)}) async-start(), calls=%async_computation.27 | async-start | bytes 1179648 | tf_op jit(solution)/shard_map/psum | solution.py:517
  685.1 100.8 %reduce-scatter.21.cloned.1.call-start = ((), (), s32[]{:S(2)}) async-start(), calls=%async_computation.20 | async-start | bytes 1966080 | tf_op jit(solution)/shard_map/reduce_scatter | solution.py:29
  700.4 137.2 %copy-start.6 = (f32[1024,192]{0,1:T(8,128)S(1)}, f32[1024,192]{0,1:T(8,128)}, u32[]{:S(2)}) copy-start(f32[1024,192]{0,1:T(8,128)} %copy-done.5) | copy-start | bytes 2359300
  701.6 136.0 %copy-start.14 = (bf16[1024,192]{0,1:T(8,128)(2,1)S(1)}, bf16[1024,192]{0,1:T(8,128)(2,1)}, u32[]{:S(2)}) copy-start(bf16[1024,192]{0,1:T(8,128)(2,1)} %param.16) | copy-start | bytes 1179652
  703.4 134.2 %copy-start.16 = (f32[1024,192]{0,1:T(8,128)S(1)}, f32[1024,192]{0,1:T(8,128)}, u32[]{:S(2)}) copy-start(f32[1024,192]{0,1:T(8,128)} %copy.154) | copy-start | bytes 2359300
  (26 other events, 580.1 us)
Sparse Core Ops, SparseCore 0:
  9.6 39.7 all-gather.7
  67.4 44.7 reduce-scatter.18
  125.2 35.2 all-gather.9
  214.1 60.3 all-gather.17
  276.4 62.1 all-gather.11
  340.0 9.6 all-gather.13
  351.2 12.0 all-gather.15
  382.0 61.4 reduce-scatter.26
  445.8 60.2 reduce-scatter.24
  582.9 37.1 all-gather.19
  638.0 18.0 reduce-scatter.30
  658.3 9.6 reduce-scatter.28
  674.2 9.3 reduce-scatter.32
  686.4 11.0 reduce-scatter.22
  700.9 47.3 all-reduce.3
  750.6 35.2 reduce-scatter.20

commit v2 on v1

v2 whole, which is shorter than its diff:
```python
import jax
import jax.numpy as jnp
from jax import lax
from jax.experimental import pallas as pl
from jax.experimental.pallas import tpu as pltpu
from jax.sharding import PartitionSpec as P

HEAD = 64
NB = 32
BUCKET = 32
SPAN = 256
TAIL = 16

EPS = 1e-06
NEG = -1e30

BF = jnp.bfloat16
F32 = jnp.float32
NN = ((1,), (0,))
NT = ((1,), (1,))
TN = ((0,), (0,))
WIDE = pltpu.CompilerParams(vmem_limit_bytes=50 * 1024 * 1024)
VMEM = pl.BlockSpec(memory_space=pltpu.VMEM)
SMEM = pl.BlockSpec(memory_space=pltpu.SMEM)


def swap(values, axis, step):
    return lax.ppermute(values, axis, [(i, i ^ step) for i in range(lax.axis_size(axis))])


def spread(values, axis):
    return [values] + [swap(values, axis, s) for s in range(1, lax.axis_size(axis))]


def exchange(blocks, axis):
    return [blocks[0]] + [swap(blocks[s], axis, s) for s in range(1, len(blocks))]


def cube_sum(values, axis, dtype):
    for bit in range((lax.axis_size(axis) - 1).bit_length()):
        sent = values.astype(dtype)
        values = sent.astype(F32) + swap(sent, axis, 1 << bit).astype(F32)
    return values


def iota(shape, dim):
    return lax.broadcasted_iota(jnp.int32, shape, dim)


def dot(a, b, dims=NN):
    return lax.dot_general(a, b, (dims, ((), ())), preferred_element_type=F32)


def shape_of(dims, dtype):
    return jax.ShapeDtypeStruct(dims, dtype)


def chunked(rows):
    return pl.BlockSpec((rows, SPAN), lambda c: (0, c))


def whole(*dims):
    return pl.BlockSpec(dims, lambda c: (0,) * len(dims))


def column_sum(values):
    return jnp.sum(values, axis=0, keepdims=True)


def token_sums(values):
    return dot(jnp.ones((8, values.shape[1]), BF), values.astype(BF), NT)


def part_rows(index, size):
    return pl.ds(pl.multiple_of(index * size, 64), size)


def slots_kernel(cap, base_ref, routes_ref, order_ref, slots_ref, hot):
    tokens, pairs = hot.shape
    experts = base_ref.shape[0]
    token = lax.shift_right_logical(order_ref[...], 1)
    second = (order_ref[...] & 1) == 1
    hot[...] = (iota((tokens, pairs), 0) == token).astype(BF)
    named = iota((experts, tokens), 0)
    chosen = jnp.where(
        second,
        dot((named == routes_ref[1:2, :]).astype(BF), hot[...]),
        dot((named == routes_ref[0:1, :]).astype(BF), hot[...]),
    )
    place = iota(chosen.shape, 1)
    upto, step = chosen, 1
    while step < pairs:
        upto = upto + jnp.where(place >= step, pltpu.roll(upto, step, 1), 0.0)
        step *= 2
    rank = column_sum((upto - chosen) * chosen)
    slot = column_sum(chosen * base_ref[...]) + rank
    kept = (rank < cap).astype(F32)
    high = jnp.floor(slot * (1 / 64))
    low = slot - 64 * high
    own = kept * second.astype(F32)
    rows = [value * side for side in (kept - own, own) for value in (high, low, 1.0)]
    rows = jnp.concatenate(rows + [rows[0] * 0.0] * 10, axis=0).astype(BF)
    found = dot(rows, hot[...], NT)
    for k in range(2):
        at = found[3 * k : 3 * k + 1, :] * 64 + found[3 * k + 1 : 3 * k + 2, :]
        at = jnp.where(found[3 * k + 2 : 3 * k + 3, :] > 0.5, at, -1.0)
        slots_ref[k : k + 1, :] = at.astype(jnp.int32)


def slot_rows(base, routes, order, cap):
    tokens = routes.shape[1]
    return pl.pallas_call(
        lambda *refs: slots_kernel(cap, *refs),
        in_specs=[VMEM] * 3,
        out_specs=VMEM,
        out_shape=shape_of((2, tokens), jnp.int32),
        scratch_shapes=[pltpu.VMEM((tokens, 2 * tokens), BF)],
        compiler_params=WIDE,
        name="slots",
    )(base, routes, order)


def project_kernel(me_ref, *refs):
    pieces = refs[:-6]
    w_ref, gain_ref, full_ref, normed_ref, proj_ref, inverse_ref = refs[-6:]
    size = pieces[0].shape[0]
    for s, piece in enumerate(pieces):
        full_ref[part_rows(me_ref[0] ^ s, size), :] = piece[...]
    x = full_ref[...].astype(F32)
    inverse = lax.rsqrt(jnp.mean(x * x, axis=0, keepdims=True) + EPS)
    normed = (x * inverse * gain_ref[...]).astype(BF)
    normed_ref[...] = normed
    inverse_ref[...] = inverse
    proj_ref[...] = dot(w_ref[...], normed, TN).astype(BF)


def project(me, pieces, w, gain):
    size, tokens = pieces[0].shape
    width, inner = w.shape
    return pl.pallas_call(
        project_kernel,
        grid=(tokens // SPAN,),
        in_specs=[SMEM] + [chunked(size)] * len(pieces) + [whole(width, inner), whole(width, 1)],
        out_specs=[chunked(width), chunked(width), chunked(inner), chunked(1)],
        out_shape=[
            shape_of((width, tokens), BF),
            shape_of((width, tokens), BF),
            shape_of((inner, tokens), BF),
            shape_of((1, tokens), F32),
        ],
        compiler_params=WIDE,
        name="project",
    )(me, *pieces, w, gain)


def hot_slots(slots_ref, k, block, size, cols=slice(None)):
    at = slots_ref[k : k + 1, cols]
    return (iota((size, at.shape[1]), 0) + block * size == at).astype(BF)


def enter_kernel(parts, me_ref, *refs):
    o_refs, w_refs, refs = refs[:parts], refs[parts : 2 * parts], refs[2 * parts :]
    (x_ref, gain_ref, router_ref, routes_ref, slots_ref) = refs[:5]
    (own_ref, inverse_ref, normed_ref, gates_ref) = refs[5:9]
    row_refs, h_all = refs[9:-1], refs[-1]
    size = own_ref.shape[0]
    tokens = x_ref.shape[1]
    width = x_ref.shape[0]
    experts = router_ref.shape[1]
    w = jnp.concatenate([ref[...] for ref in w_refs], axis=0)
    for c in range(tokens // SPAN):
        cols = slice(c * SPAN, (c + 1) * SPAN)
        o = jnp.concatenate([ref[:, cols] for ref in o_refs], axis=0)
        h = x_ref[:, cols].astype(F32) + dot(w, o, TN)
        h_all[:, cols] = h
        inverse = lax.rsqrt(jnp.mean(h * h, axis=0, keepdims=True) + EPS)
        normed = (h * inverse * gain_ref[...]).astype(BF)
        inverse_ref[:, cols] = inverse
        normed_ref[:, cols] = normed
        logits = dot(router_ref[...], normed, TN)
        named = iota((experts, SPAN), 0)
        one, two = [
            column_sum(jnp.where(named == routes_ref[k : k + 1, cols], logits, 0.0)) for k in range(2)
        ]
        top = jnp.maximum(one, two)
        one, two = jnp.exp(one - top), jnp.exp(two - top)
        total = one + two
        gates_ref[0:1, cols] = one / total
        gates_ref[1:2, cols] = two / total
    own_ref[...] = h_all[part_rows(me_ref[0], size), :]
    gate_rows = []
    for k in range(2):
        gate = gates_ref[k : k + 1, :]
        high = gate.astype(BF)
        rest = (gate - high.astype(F32)).astype(BF)
        gate_rows.append(jnp.concatenate([high, rest, jnp.zeros((TAIL - 2, tokens), BF)], axis=0))
    for b, ref in enumerate(row_refs):
        hots = [hot_slots(slots_ref, k, b, ref.shape[1]) for k in range(2)]
        ref[:width, :] = dot(normed_ref[...], hots[0] + hots[1], NT).astype(BF)
        ref[width:, :] = (dot(gate_rows[0], hots[0], NT) + dot(gate_rows[1], hots[1], NT)).astype(BF)


def enter(me, o_pieces, w_pieces, x, gain, router, routes, slots, blocks, block):
    size, tokens = o_pieces[0].shape
    width = x.shape[0]
    parts = len(o_pieces)
    return pl.pallas_call(
        lambda *refs: enter_kernel(parts, *refs),
        in_specs=[SMEM] + [VMEM] * (2 * parts + 5),
        out_specs=[VMEM] * (4 + blocks),
        out_shape=[
            shape_of((width // parts, tokens), F32),
            shape_of((1, tokens), F32),
            shape_of((width, tokens), BF),
            shape_of((2, tokens), F32),
        ]
        + [shape_of((width + TAIL, block), BF)] * blocks,
        scratch_shapes=[pltpu.VMEM((width, tokens), F32)],
        compiler_params=WIDE,
        name="enter",
    )(me, *o_pieces, *w_pieces, x, gain, router, routes, slots)


def send_kernel(parts, me_ref, *refs):
    pieces, slots_ref, full_ref, row_refs = refs[:parts], refs[parts], refs[parts + 1], refs[parts + 2 :]
    size = pieces[0].shape[0]
    for s, piece in enumerate(pieces):
        full_ref[part_rows(me_ref[0] ^ s, size), :] = piece[...]
    for b, ref in enumerate(row_refs):
        hot = hot_slots(slots_ref, 0, b, ref.shape[1]) + hot_slots(slots_ref, 1, b, ref.shape[1])
        ref[...] = dot(full_ref[...], hot, NT).astype(BF)


def send_rows(me, pieces, slots, blocks, block):
    size, tokens = pieces[0].shape
    width = size * len(pieces)
    return pl.pallas_call(
        lambda *refs: send_kernel(len(pieces), *refs),
        in_specs=[SMEM] + [VMEM] * (len(pieces) + 1),
        out_specs=[VMEM] * (1 + blocks),
        out_shape=[shape_of((width, tokens), BF)] + [shape_of((width, block), BF)] * blocks,
        compiler_params=WIDE,
        name="send",
    )(me, *pieces, slots)


def expert_kernel(count, *refs):
    rows, cots = refs[:count], refs[count : 2 * count]
    w_in_ref, w_out_ref = refs[2 * count : 2 * count + 2]
    outs = refs[2 * count + 2 : 3 * count + 2]
    act_ref, pre_ref, sent_ref = refs[3 * count + 2 :]
    width = w_in_ref.shape[0]
    scale = (2 / jnp.pi) ** 0.5
    for b in range(count):
        block = rows[b].shape[1]
        cols = slice(b * block, (b + 1) * block)
        gate = column_sum(rows[b][width : width + 2, :].astype(F32))
        cot = cots[b][...]
        sent_ref[:, cols] = (cot.astype(F32) * gate).astype(BF)
        pre = dot(w_in_ref[...], rows[b][:width, :], TN)
        square = pre * pre
        bend = jnp.tanh(scale * pre * (1 + 0.044715 * square))
        half = 0.5 * (1 + bend)
        act = (pre * half).astype(BF)
        slope = half + 0.5 * pre * (1 - bend * bend) * (scale * (1 + 3 * 0.044715 * square))
        act_ref[:, cols] = act
        back = dot(w_out_ref[...], cot)
        gate_grad = column_sum(act.astype(F32) * back)
        pre_grad = (slope * back * gate).astype(BF)
        pre_ref[:, cols] = pre_grad
        outs[b][:width, :] = dot(w_in_ref[...], pre_grad).astype(BF)
        high = gate_grad.astype(BF)
        rest = (gate_grad - high.astype(F32)).astype(BF)
        outs[b][width:, :] = jnp.concatenate([high, rest, jnp.zeros((TAIL - 2, block), BF)], axis=0)


def expert(rows, cots, w_in, w_out):
    count, block = len(rows), rows[0].shape[1]
    width, hidden = w_in.shape
    return pl.pallas_call(
        lambda *refs: expert_kernel(count, *refs),
        in_specs=[VMEM] * (2 * count + 2),
        out_specs=[VMEM] * (count + 3),
        out_shape=[shape_of((width + TAIL, block), BF)] * count
        + [shape_of((hidden, count * block), BF)] * 2
        + [shape_of((width, count * block), BF)],
        compiler_params=WIDE,
        name="expert",
    )(*rows, *cots, w_in, w_out)


def expert_out_kernel(act_ref, w_out_ref, *outs):
    for b, out in enumerate(outs):
        block = out.shape[1]
        out[...] = dot(w_out_ref[...], act_ref[:, b * block : (b + 1) * block], TN).astype(BF)


def expert_out(act, w_out, count):
    block = act.shape[1] // count
    return pl.pallas_call(
        expert_out_kernel,
        in_specs=[VMEM] * 2,
        out_specs=[VMEM] * count,
        out_shape=[shape_of((w_out.shape[1], block), BF)] * count,
        compiler_params=WIDE,
        name="expert_out",
    )(act, w_out)


def expert_weights_kernel(count, side_ref, *refs):
    rows = refs[:count]
    act_ref, pre_ref, sent_ref, in_keep, in_send, out_keep, out_send = refs[count:]
    half = in_keep.shape[0]
    block = rows[0].shape[1]
    for in_ref, out_ref, side in (
        (in_keep, out_keep, side_ref[0]),
        (in_send, out_send, 1 - side_ref[0]),
    ):
        at = part_rows(side, half)
        total = 0.0
        for b in range(count):
            total = total + dot(rows[b][at, :], pre_ref[:, b * block : (b + 1) * block], NT)
        in_ref[...] = total.astype(in_ref.dtype)
        out_ref[...] = dot(act_ref[...], sent_ref[at, :], NT).astype(out_ref.dtype)


def expert_weights(side, rows, act, pre, sent):
    width, hidden = sent.shape[0], act.shape[0]
    return pl.pallas_call(
        lambda *refs: expert_weights_kernel(len(rows), *refs),
        in_specs=[SMEM] + [VMEM] * (len(rows) + 3),
        out_specs=[VMEM] * 4,
        out_shape=[
            shape_of((width // 2, hidden), F32),
            shape_of((width // 2, hidden), BF),
            shape_of((hidden, width // 2), F32),
            shape_of((hidden, width // 2), BF),
        ],
        compiler_params=WIDE,
        name="expert_weights",
    )(side, *rows, act, pre, sent)


def collect_kernel(blocks, parts, *refs):
    row_refs, w_refs = refs[:blocks], refs[blocks : blocks + parts]
    slots_ref, inverse_ref, gain_ref, normed_ref = refs[blocks + parts : blocks + parts + 4]
    part_ref, small_ref, sums_ref = refs[blocks + parts + 4 : blocks + parts + 7]
    out_refs = refs[blocks + parts + 7 :]
    width = gain_ref.shape[0]
    total = 0.0
    gate_grads = [0.0, 0.0]
    for b, ref in enumerate(row_refs):
        hots = [hot_slots(slots_ref, k, b, ref.shape[1]) for k in range(2)]
        total = total + dot(ref[:width, :], hots[0] + hots[1])
        for k in range(2):
            gate_grads[k] = gate_grads[k] + dot(ref[width:, :], hots[k])
    for k in range(2):
        small_ref[k : k + 1, :] = column_sum(gate_grads[k][:2, :])
    product = total * normed_ref[...].astype(F32)
    small_ref[2:3, :] = column_sum(product)
    small_ref[3:, :] = jnp.zeros((5, SPAN), F32)

    @pl.when(pl.program_id(0) == 0)
    def _():
        sums_ref[...] = jnp.zeros_like(sums_ref)

    sums_ref[...] += token_sums(product)
    part = (total * inverse_ref[...] * gain_ref[...]).astype(BF)
    part_ref[...] = part
    for w_ref, out_ref in zip(w_refs, out_refs):
        out_ref[...] = dot(w_ref[...], part).astype(BF)


def collect(rows, w_pieces, slots, inverse, gain, normed):
    width, tokens = normed.shape
    blocks, parts = len(rows), len(w_pieces)
    inner = w_pieces[0].shape[0]
    return pl.pallas_call(
        lambda *refs: collect_kernel(blocks, parts, *refs),
        grid=(tokens // SPAN,),
        in_specs=[whole(*rows[0].shape)] * blocks
        + [whole(inner, width)] * parts
        + [chunked(2), chunked(1), whole(width, 1), chunked(width)],
        out_specs=[chunked(width), chunked(8), whole(8, width)] + [chunked(inner)] * parts,
        out_shape=[shape_of((width, tokens), BF), shape_of((8, tokens), F32), shape_of((8, width), F32)]
        + [shape_of((inner, tokens), BF)] * parts,
        compiler_params=WIDE,
        name="collect",
    )(*rows, *w_pieces, slots, inverse, gain, normed)


def turn_kernel(parts, me_ref, *refs):
    pieces, smalls, refs = refs[:parts], refs[parts : 2 * parts], refs[2 * parts :]
    (w_ref, gates_ref, routes_ref, normed_ref, cot_ref, inverse_ref, gain_ref, router_ref) = refs[:8]
    (do_ref, rest_ref, own_ref, router_out, sums_ref, scratch) = refs[8:]
    width, experts = router_ref.shape
    size = own_ref.shape[0]
    small = smalls[0][...]
    for ref in smalls[1:]:
        small = small + ref[...]
    grads = [small[k : k + 1, :] for k in range(2)]
    gates = [gates_ref[k : k + 1, :] for k in range(2)]
    mean = gates[0] * grads[0] + gates[1] * grads[1]
    logits = 0.0
    for k in range(2):
        hot = iota((experts, SPAN), 0) == routes_ref[k : k + 1, :]
        logits = logits + jnp.where(hot, gates[k] * (grads[k] - mean), 0.0)
    logits = logits.astype(BF)
    routed = dot(router_ref[...], logits)
    normed = normed_ref[...].astype(F32)
    product = routed * normed
    level = (small[2:3, :] + column_sum(product)) / width
    gain = gain_ref[...]
    rest = cot_ref[...].astype(F32) + inverse_ref[...] * (gain * routed - level * (normed / gain))
    scratch[...] = rest
    rest = rest.astype(BF)
    rest_ref[...] = rest
    own_ref[...] = scratch[part_rows(me_ref[0], size), :]
    do = dot(w_ref[...], rest)
    for ref in pieces:
        do = do + ref[...].astype(F32)
    do_ref[...] = do.astype(BF)

    @pl.when(pl.program_id(0) == 0)
    def _():
        router_out[...] = jnp.zeros_like(router_out)
        sums_ref[...] = jnp.zeros_like(sums_ref)

    @pl.when(me_ref[0] == 0)
    def _():
        router_out[...] += dot(logits, normed_ref[...], NT)
        sums_ref[...] += token_sums(product)


def turn(me, pieces, smalls, w, gates, routes, normed, cot, inverse, gain, router):
    width, tokens = normed.shape
    parts = len(pieces)
    inner = w.shape[0]
    experts = router.shape[1]
    return pl.pallas_call(
        lambda *refs: turn_kernel(parts, *refs),
        grid=(tokens // SPAN,),
        in_specs=[SMEM]
        + [chunked(inner)] * parts
        + [chunked(8)] * parts
        + [
            whole(inner, width), chunked(2), chunked(2), chunked(width), chunked(width),
            chunked(1), whole(width, 1), whole(width, experts),
        ],
        out_specs=[
            chunked(inner), chunked(width), chunked(width // parts), whole(experts, width), whole(8, width),
        ],
        out_shape=[
            shape_of((inner, tokens), BF),
            shape_of((width, tokens), BF),
            shape_of((width // parts, tokens), F32),
            shape_of((experts, width), F32),
            shape_of((8, width), F32),
        ],
        scratch_shapes=[pltpu.VMEM((width, SPAN), F32)],
        compiler_params=WIDE,
        name="turn",
    )(me, *pieces, *smalls, w, gates, routes, normed, cot, inverse, gain, router)


def merge_kernel(blocks, me_ref, *refs):
    row_refs, slots_ref, gates_ref = refs[:blocks], refs[blocks], refs[blocks + 1]
    outs, scratch = refs[blocks + 2 : -1], refs[-1]
    total = 0.0
    for k in range(2):
        picked = 0.0
        for b, ref in enumerate(row_refs):
            picked = picked + dot(ref[...], hot_slots(slots_ref, k, b, ref.shape[1]))
        total = total + gates_ref[k : k + 1, :] * picked
    scratch[...] = total
    for s, out in enumerate(outs):
        out[...] = scratch[part_rows(me_ref[0] ^ s, out.shape[0]), :].astype(BF)


def merge(me, rows, slots, gates, parts):
    width, tokens = rows[0].shape[0], slots.shape[1]
    return pl.pallas_call(
        lambda *refs: merge_kernel(len(rows), *refs),
        grid=(tokens // SPAN,),
        in_specs=[SMEM] + [whole(*rows[0].shape)] * len(rows) + [chunked(2), chunked(2)],
        out_specs=[chunked(width // parts)] * parts,
        out_shape=[shape_of((width // parts, tokens), BF)] * parts,
        scratch_shapes=[pltpu.VMEM((width, SPAN), F32)],
        compiler_params=WIDE,
        name="merge",
    )(me, *rows, slots, gates)


def out_weights_kernel(parts, side_ref, *refs):
    o_refs, part_ref, rest_ref, keep_ref, send_ref = refs[:parts], *refs[parts:]
    size = o_refs[0].shape[0]
    half = keep_ref.shape[1]
    for out, side in ((keep_ref, side_ref[0]), (send_ref, 1 - side_ref[0])):
        at = part_rows(side, half)
        for s, o_ref in enumerate(o_refs):
            total = dot(o_ref[...], part_ref[at, :], NT)
            if s == 0:
                total = total + dot(o_ref[...], rest_ref[at, :], NT)
            out[s * size : (s + 1) * size, :] = total.astype(BF)


def out_weights(side, o_pieces, part, rest):
    size, width = o_pieces[0].shape[0], part.shape[0]
    return pl.pallas_call(
        lambda *refs: out_weights_kernel(len(o_pieces), *refs),
        in_specs=[SMEM] + [VMEM] * (len(o_pieces) + 2),
        out_specs=[VMEM] * 2,
        out_shape=[shape_of((size * len(o_pieces), width // 2), BF)] * 2,
        compiler_params=WIDE,
        name="out_weights",
    )(side, *o_pieces, part, rest)


def leave_kernel(parts, me_ref, *refs):
    dq_ref, dk_ref, dv_ref, dkp_ref, dvp_ref, w_ref, part_ref, normed_ref, inverse_ref, gain_ref = refs[:10]
    grad_ref, small_ref, sums_ref = refs[10:13]
    outs, scratch = refs[13:-1], refs[-1]
    own = [dq_ref[...]] + [
        (a[...].astype(F32) + b[...].astype(F32)).astype(BF) for a, b in ((dk_ref, dkp_ref), (dv_ref, dvp_ref))
    ]
    grad = jnp.concatenate(own, axis=0)
    grad_ref[...] = grad
    back = dot(w_ref[...], grad)
    product = back * normed_ref[...].astype(F32)
    small_ref[...] = jnp.broadcast_to(column_sum(product), small_ref.shape)

    @pl.when(pl.program_id(0) == 0)
    def _():
        sums_ref[...] = jnp.zeros_like(sums_ref)

    sums_ref[...] += token_sums(product)
    scratch[...] = part_ref[...].astype(F32) + back * inverse_ref[...] * gain_ref[...]
    for s, out in enumerate(outs):
        out[...] = scratch[part_rows(me_ref[0] ^ s, out.shape[0]), :].astype(BF)


def leave(me, dq, dk, dv, dkp, dvp, w, part, normed, inverse, gain, parts):
    width, tokens = normed.shape
    inner = dq.shape[0]
    return pl.pallas_call(
        lambda *refs: leave_kernel(parts, *refs),
        grid=(tokens // SPAN,),
        in_specs=[SMEM]
        + [chunked(inner)] * 5
        + [whole(*w.shape), chunked(width), chunked(width), chunked(1), whole(width, 1)],
        out_specs=[chunked(3 * inner), chunked(8), whole(8, width)] + [chunked(width // parts)] * parts,
        out_shape=[shape_of((3 * inner, tokens), BF), shape_of((8, tokens), F32), shape_of((8, width), F32)]
        + [shape_of((width // parts, tokens), BF)] * parts,
        scratch_shapes=[pltpu.VMEM((width, SPAN), F32)],
        compiler_params=WIDE,
        name="leave",
    )(me, dq, dk, dv, dkp, dvp, w, part, normed, inverse, gain)


def in_weights_kernel(side_ref, normed_ref, grad_ref, keep_ref, send_ref):
    half = keep_ref.shape[0]
    keep_ref[...] = dot(normed_ref[part_rows(side_ref[0], half), :], grad_ref[...], NT).astype(BF)
    send_ref[...] = dot(normed_ref[part_rows(1 - side_ref[0], half), :], grad_ref[...], NT).astype(BF)


def in_weights(side, normed, grad):
    dims = (normed.shape[0] // 2, grad.shape[0])
    return pl.pallas_call(
        in_weights_kernel,
        in_specs=[SMEM, VMEM, VMEM],
        out_specs=[VMEM] * 2,
        out_shape=[shape_of(dims, BF)] * 2,
        compiler_params=WIDE,
        name="in_weights",
    )(side, normed, grad)


def fill_bias(near_ref, far_ref, table_ref):
    low = (iota((BUCKET, SPAN), 1) & (BUCKET - 1)) >= iota((BUCKET, SPAN), 0)
    for c in range(table_ref.shape[0] // BUCKET):
        table_ref[c * BUCKET : (c + 1) * BUCKET, :] = jnp.where(
            low, near_ref[0, c : c + 1, :], far_ref[0, c : c + 1, :]
        )


def split_bias(table_ref, count):
    table = table_ref[:count, :]
    high = table.astype(jnp.bfloat16)
    return high, (table - high.astype(jnp.float32)).astype(jnp.bfloat16)


def attend_kernel(
    cont_ref, q_ref, k_ref, v_ref, kp_ref, vp_ref, first_ref, near_ref, far_ref,
    o_ref, log_ref, table, key_own, key_prev, val_own, val_prev,
):
    count = q_ref.shape[1]
    cont = cont_ref[0] == 1
    fill_bias(near_ref, far_ref, table)
    key_own[...] = k_ref[...].T
    ones = jnp.ones((16, count), jnp.bfloat16)
    val_own[:HEAD, :] = v_ref[...]
    val_own[HEAD:, :] = ones

    def finish(o, top, cols):
        total = o[HEAD : HEAD + 1, :]
        o_ref[:, cols] = (o[:HEAD, :] / total).astype(jnp.bfloat16)
        log_ref[0, :, cols] = top + jnp.log(total)

    @pl.when(jnp.logical_not(cont))
    def _():
        for b in range(count // SPAN):
            cols = slice(b * SPAN, (b + 1) * SPAN)
            keys = (b + 1) * SPAN
            q = q_ref[:, cols] * jnp.bfloat16(HEAD**-0.5)
            s = dot(key_own[:keys, :], q) + table[count - b * SPAN : count + SPAN, :]
            s = jnp.where(iota((keys, SPAN), 0) <= iota((keys, SPAN), 1) + b * SPAN, s, NEG)
            top = jnp.max(s, axis=0, keepdims=True)
            p = jnp.exp(s - top).astype(jnp.bfloat16)
            finish(dot(val_own[:, :keys], p), top, cols)

    @pl.when(cont)
    def _():
        high, rest = split_bias(table, count)
        key_prev[:, :SPAN] = high
        key_prev[:, SPAN : 2 * SPAN] = rest
        key_prev[:, 2 * SPAN :] = kp_ref[...].T
        val_prev[:HEAD, :] = vp_ref[...]
        val_prev[HEAD:, :] = ones
        for b in range(count // SPAN):
            cols = slice(b * SPAN, (b + 1) * SPAN)
            start = max(b - 1, 0) * SPAN
            rows = slice(start, (b + 1) * SPAN)
            keys = (b + 1) * SPAN - start
            q = q_ref[:, cols] * jnp.bfloat16(HEAD**-0.5)
            first = first_ref[:, cols]
            place = iota((1, SPAN), 1) + b * SPAN
            hot = (iota((SPAN, SPAN), 0) == place - first).astype(jnp.bfloat16)
            s1 = dot(key_prev[...], jnp.concatenate([hot, hot, q], axis=0))
            s2 = dot(key_own[rows, :], q) + table[count + start - b * SPAN : count + SPAN, :]
            at = iota((keys, SPAN), 0) + start
            s2 = jnp.where((at <= place) & (at >= first), s2, NEG)
            top = jnp.maximum(
                jnp.max(s1, axis=0, keepdims=True), jnp.max(s2, axis=0, keepdims=True)
            )
            p1 = jnp.exp(s1 - top).astype(jnp.bfloat16)
            p2 = jnp.exp(s2 - top).astype(jnp.bfloat16)
            finish(dot(val_prev[...], p1) + dot(val_own[:, rows], p2), top, cols)


def attend(cont, proj, prev, first, near, far):
    heads, count = proj.shape[0] // (3 * HEAD), proj.shape[1]
    part = lambda k: pl.BlockSpec((HEAD, count), lambda h: (h + k * heads, 0))
    table = pl.BlockSpec((1,) + near.shape[1:], lambda h: (h, 0, 0))
    return pl.pallas_call(
        attend_kernel,
        grid=(heads,),
        in_specs=[
            pl.BlockSpec(memory_space=pltpu.SMEM),
            part(0), part(1), part(2), part(0), part(1),
            pl.BlockSpec((1, count), lambda h: (0, 0)),
            table, table,
        ],
        out_specs=[part(0), pl.BlockSpec((1, 1, count), lambda h: (h, 0, 0))],
        out_shape=[
            jax.ShapeDtypeStruct((heads * HEAD, count), jnp.bfloat16),
            jax.ShapeDtypeStruct((heads, 1, count), jnp.float32),
        ],
        scratch_shapes=[
            pltpu.VMEM((2 * count, SPAN), jnp.float32),
            pltpu.VMEM((count, HEAD), jnp.bfloat16),
            pltpu.VMEM((count, HEAD + 2 * SPAN), jnp.bfloat16),
            pltpu.VMEM((HEAD + 16, count), jnp.bfloat16),
            pltpu.VMEM((HEAD + 16, count), jnp.bfloat16),
        ],
        compiler_params=WIDE,
        name="attend",
    )(cont, proj, proj, proj, prev, prev, first, near, far)


def attend_back_kernel(
    cont_ref, q_ref, k_ref, v_ref, kp_ref, vp_ref, first_ref, near_ref, far_ref, o_ref, log_ref, do_ref,
    dq_ref, dk_ref, dv_ref, dkp_ref, dvp_ref, sum_near_ref, sum_far_ref,
    table, key_own, key_prev, val_own, val_prev, q_cat, q_nat, do_nat, hot_nat, dtable, dq, dk, dv,
):
    count = q_ref.shape[1]
    blocks = count // SPAN
    cont = cont_ref[0] == 1
    fill_bias(near_ref, far_ref, table)
    key_own[...] = k_ref[...].T
    val_own[...] = v_ref[...].T
    q = q_ref[...] * jnp.bfloat16(HEAD**-0.5)
    q_cat[2 * SPAN :, :] = q
    q_nat[...] = q.T
    do_nat[...] = do_ref[...].T
    dtable[...] = jnp.zeros_like(dtable)
    dq[...] = jnp.zeros_like(dq)
    dk[...] = jnp.zeros_like(dk)
    dv[...] = jnp.zeros_like(dv)
    delta = jnp.sum(
        do_ref[...].astype(jnp.float32) * o_ref[...].astype(jnp.float32), axis=0, keepdims=True
    )

    def tile(kb, qb):
        rows = slice(kb * SPAN, (kb + 1) * SPAN)
        cols = slice(qb * SPAN, (qb + 1) * SPAN)
        where = slice(count + (kb - qb) * SPAN, count + (kb - qb + 1) * SPAN)
        s = dot(key_own[rows, :], q_cat[2 * SPAN :, cols]) + table[where, :]
        at = iota((SPAN, SPAN), 0) + kb * SPAN
        live = (at <= iota((SPAN, SPAN), 1) + qb * SPAN) & (at >= first_ref[:, cols])
        p = jnp.exp(jnp.where(live, s, NEG) - log_ref[0, :, cols])
        dp = dot(val_own[rows, :], do_ref[:, cols])
        ds = p * (dp - delta[:, cols])
        dtable[where, :] += ds
        ds = ds.astype(jnp.bfloat16)
        dk[rows, :] += dot(ds, q_nat[cols, :])
        dv[rows, :] += dot(p.astype(jnp.bfloat16), do_nat[cols, :])
        dq[:, cols] += dot(k_ref[:, rows], ds)

    for kb in range(blocks):
        for qb in range(kb, min(kb + 2, blocks)):
            tile(kb, qb)

    @pl.when(jnp.logical_not(cont))
    def _():
        for kb in range(blocks):
            for qb in range(kb + 2, blocks):
                tile(kb, qb)

    @pl.when(cont)
    def _():
        high, rest = split_bias(table, count)
        key_prev[:, :SPAN] = high
        key_prev[:, SPAN : 2 * SPAN] = rest
        key_prev[:, 2 * SPAN :] = kp_ref[...].T
        val_prev[...] = vp_ref[...].T
        hot = (iota((SPAN, count), 0) == iota((1, count), 1) - first_ref[...]).astype(jnp.bfloat16)
        q_cat[:SPAN, :] = hot
        q_cat[SPAN : 2 * SPAN, :] = hot
        hot_nat[...] = hot.T

        for kb in range(blocks):
            rows = slice(kb * SPAN, (kb + 1) * SPAN)
            s = dot(key_prev[rows, :], q_cat[...])
            p = jnp.exp(s - log_ref[0])
            dp = dot(val_prev[rows, :], do_ref[...])
            ds = (p * (dp - delta)).astype(jnp.bfloat16)
            dkp_ref[:, rows] = dot(ds, q_nat[...]).astype(jnp.bfloat16).T
            dvp_ref[:, rows] = dot(p.astype(jnp.bfloat16), do_nat[...]).astype(jnp.bfloat16).T
            dtable[rows, :] += dot(ds, hot_nat[...])
            dq[...] += dot(kp_ref[:, rows], ds)

    dq_ref[...] = (dq[...] * HEAD**-0.5).astype(jnp.bfloat16)
    dk_ref[...] = dk[...].astype(jnp.bfloat16).T
    dv_ref[...] = dv[...].astype(jnp.bfloat16).T
    low = (iota((BUCKET, SPAN), 1) & (BUCKET - 1)) >= iota((BUCKET, SPAN), 0)
    for c in range(2 * count // BUCKET):
        part = dtable[c * BUCKET : (c + 1) * BUCKET, :]
        near = jnp.sum(jnp.where(low, part, 0.0), axis=0, keepdims=True)
        sum_near_ref[0, c : c + 1, :] = near
        sum_far_ref[0, c : c + 1, :] = jnp.sum(part, axis=0, keepdims=True) - near


def attend_back(cont, proj, prev, first, near, far, o, log, do):
    heads, count = proj.shape[0] // (3 * HEAD), proj.shape[1]
    part = lambda k: pl.BlockSpec((HEAD, count), lambda h: (h + k * heads, 0))
    table = pl.BlockSpec((1,) + near.shape[1:], lambda h: (h, 0, 0))
    grad = jax.ShapeDtypeStruct((heads * HEAD, count), jnp.bfloat16)
    sums = jax.ShapeDtypeStruct(near.shape, jnp.float32)
    return pl.pallas_call(
        attend_back_kernel,
        grid=(heads,),
        in_specs=[
            pl.BlockSpec(memory_space=pltpu.SMEM),
            part(0), part(1), part(2), part(0), part(1),
            pl.BlockSpec((1, count), lambda h: (0, 0)),
            table, table, part(0),
            pl.BlockSpec((1, 1, count), lambda h: (h, 0, 0)),
            part(0),
        ],
        out_specs=[part(0)] * 5 + [table] * 2,
        out_shape=[grad] * 5 + [sums] * 2,
        scratch_shapes=[
            pltpu.VMEM((2 * count, SPAN), jnp.float32),
            pltpu.VMEM((count, HEAD), jnp.bfloat16),
            pltpu.VMEM((count, HEAD + 2 * SPAN), jnp.bfloat16),
            pltpu.VMEM((count, HEAD), jnp.bfloat16),
            pltpu.VMEM((count, HEAD), jnp.bfloat16),
            pltpu.VMEM((HEAD + 2 * SPAN, count), jnp.bfloat16),
            pltpu.VMEM((count, HEAD), jnp.bfloat16),
            pltpu.VMEM((count, HEAD), jnp.bfloat16),
            pltpu.VMEM((count, SPAN), jnp.bfloat16),
            pltpu.VMEM((2 * count, SPAN), jnp.float32),
            pltpu.VMEM((HEAD, count), jnp.float32),
            pltpu.VMEM((count, HEAD), jnp.float32),
            pltpu.VMEM((count, HEAD), jnp.float32),
        ],
        compiler_params=WIDE,
        name="attend_back",
    )(cont, proj, proj, proj, prev, prev, first, near, far, o, log, do)


def bias_levels(bias, count):
    rows, lanes = 2 * count // BUCKET, SPAN // BUCKET
    step = jnp.arange(lanes)[None, :] - jnp.arange(rows)[:, None] + rows // 2
    names = jnp.arange(NB)
    near_hot = (jnp.clip(step, 0, NB - 1)[..., None] == names).astype(jnp.float32)
    far_hot = (jnp.clip(step - 1, 0, NB - 1)[..., None] == names).astype(jnp.float32)
    return near_hot, far_hot


def bias_tables(bias, count):
    out = []
    for hot in bias_levels(bias, count):
        level = jnp.sum(hot[None] * bias[:, None, None, :], axis=-1)
        out.append(jnp.repeat(level, BUCKET, axis=2))
    return out


def bias_totals(sum_near, sum_far, count):
    total = 0.0
    for hot, sums in zip(bias_levels(None, count), (sum_near, sum_far)):
        level = jnp.sum(sums.reshape(sums.shape[0], sums.shape[1], -1, BUCKET), axis=-1)
        total = total + jnp.sum(level[..., None] * hot[None], axis=(1, 2))
    return total


def body(
    block_entry_rows,
    cotangent,
    gain_one,
    w_qkv,
    w_out_attn,
    rel_bias,
    gain_two,
    router,
    w_in,
    w_out,
    routes,
    slot_order,
    cont_ids,
):
    tokens, feats = block_entry_rows.shape
    width, experts = router.shape
    per_dev = w_in.shape[0]
    owners = experts // per_dev
    cap = 2 * tokens // experts
    inner = w_qkv.shape[2]
    heads = inner // HEAD
    parts = lax.axis_size("mx")
    my_part, my_owner, my_side = lax.axis_index("mx"), lax.axis_index("dp"), lax.axis_index("my")
    me, side = my_part.astype(jnp.int32).reshape(1), my_side.astype(jnp.int32).reshape(1)
    is_cont = my_side == 1
    by_owner = cap % 128 == 0
    count, block = (owners, cap) if by_owner else (1, owners * cap)

    def trade(rows):
        if by_owner:
            return exchange(rows, "dp")
        return [lax.all_to_all(rows[0], "dp", split_axis=1, concat_axis=1, tiled=True)]

    x_own, c_own = block_entry_rows.T, cotangent.T
    x_pieces = spread(x_own, "mx")
    qkv_full = lax.all_gather(w_qkv, "my", axis=0, tiled=True).reshape(width, 3 * inner)
    out_own = lax.all_gather(w_out_attn, "my", axis=1, tiled=True)
    win_full = lax.all_gather(w_in, "my", axis=1, tiled=True)
    wout_full = lax.all_gather(w_out, "my", axis=2, tiled=True)
    gain_a, gain_b = gain_one[:, None], gain_two[:, None]

    ids = jnp.arange(experts)
    owner = ids // per_dev
    owner = owner ^ my_owner if by_owner else owner
    base = (((ids % per_dev) * owners + owner) * cap).astype(F32)[:, None]
    routes = routes.T
    slots = slot_rows(base, routes, slot_order, cap)

    index = jnp.arange(tokens, dtype=jnp.int32)
    same_seg = cont_ids[0][:, None] == cont_ids[0][None, :]
    first = jnp.min(jnp.where(same_seg, index[:, None], tokens), axis=0, keepdims=True)
    first = jnp.where(is_cont, first, 0)
    bias_own = lax.dynamic_slice_in_dim(rel_bias, my_part * heads, heads, 0)
    near, far = bias_tables(bias_own, tokens)

    x_full, normed_one, proj, inverse_one = project(me, x_pieces, qkv_full, gain_a)
    earlier = lax.ppermute(proj[inner:], "my", [(0, 1)])
    geometry = (side, proj, earlier, first, near, far)
    o_own, logs = attend(*geometry)
    o_pieces = spread(o_own, "mx")
    out_pieces = spread(out_own, "mx")
    c_pieces = spread(c_own, "mx")
    c_full, *c_rows = send_rows(me, c_pieces, slots, per_dev * count, block)
    c_rows = [trade(c_rows[j * count : (j + 1) * count]) for j in range(per_dev)]
    h_own, inverse_two, normed_two, gates, *rows = enter(
        me, o_pieces, out_pieces, x_full, gain_b, router, routes, slots, per_dev * count, block
    )
    rows = [trade(rows[j * count : (j + 1) * count]) for j in range(per_dev)]

    back_rows, kept = [], []
    for j in range(per_dev):
        *back, act, pre, sent = expert(rows[j], c_rows[j], win_full[j], wout_full[j])
        back_rows += trade(back)
        kept.append((act, pre, sent))
    part, small, gain_b_sums, *do_blocks = collect(
        back_rows, out_pieces, slots, inverse_two, gain_b, normed_two
    )
    do_pieces = exchange(do_blocks, "mx")
    smalls = spread(small, "mx")
    do, rest, rest_own, router_sums, gain_b_rest = turn(
        me, do_pieces, smalls, out_own, gates, routes, normed_two, c_full, inverse_two, gain_b, router
    )

    expert_rows, win_grads, wout_grads = [], [], []
    for j, (act, pre, sent) in enumerate(kept):
        expert_rows += trade(expert_out(act, wout_full[j], count))
        in_keep, in_send, out_keep, out_send = expert_weights(side, rows[j], act, pre, sent)
        win_grads.append(in_keep + swap(in_send, "my", 1).astype(F32))
        wout_grads.append(out_keep + swap(out_send, "my", 1).astype(F32))
    mixed = exchange(merge(me, expert_rows, slots, gates, parts), "mx")
    block_output = h_own
    for piece in mixed:
        block_output = block_output + piece.astype(F32)

    dq, dk, dv, dkp, dvp, near_sums, far_sums = attend_back(*geometry, o_own, logs, do)
    dkp, dvp = lax.ppermute((dkp, dvp), "my", [(1, 0)])
    grad, small, gain_a_sums, *x_blocks = leave(
        me, dq, dk, dv, dkp, dvp, qkv_full, part, normed_one, inverse_one, gain_a, parts
    )
    x_blocks = exchange(x_blocks, "mx")
    level = sum(piece[:1] for piece in spread(small, "mx")) / width
    d_x = rest_own - level * inverse_one * inverse_one * x_own.astype(F32)
    for piece in x_blocks:
        d_x = d_x + piece.astype(F32)

    keep, send = out_weights(side, o_pieces, part, rest)
    keep = (keep.astype(F32) + swap(send, "my", 1).astype(F32)).astype(BF)
    keep = exchange([keep[s * inner : (s + 1) * inner] for s in range(parts)], "mx")
    d_w_out_attn = cube_sum(sum(piece.astype(F32) for piece in keep), "dp", BF)
    keep, send = in_weights(side, normed_one, grad)
    d_w_qkv = cube_sum(keep.astype(F32) + swap(send, "my", 1).astype(F32), "dp", BF)

    bias_grad = lax.dynamic_update_slice_in_dim(
        jnp.zeros(rel_bias.shape, F32), bias_totals(near_sums, far_sums, tokens), my_part * heads, 0
    ).reshape(1, -1)
    bias_grad = jnp.pad(bias_grad, ((0, 0), (0, width - bias_grad.shape[1])))
    sums = jnp.concatenate([gain_a_sums[:1], gain_b_sums[:1] + gain_b_rest[:1], bias_grad, router_sums], axis=0)
    for axis in ("my", "dp", "mx"):
        sums = cube_sum(sums, axis, F32)
    return (
        block_output.T,
        d_x.T,
        d_w_qkv.reshape(width // 2, 3, inner),
        d_w_out_attn,
        sums[2, : rel_bias.size].reshape(rel_bias.shape),
        sums[0] / gain_one,
        sums[1] / gain_two,
        sums[3:].T,
        jnp.stack(win_grads),
        jnp.stack(wout_grads),
    )


def solution(mesh):
    return jax.shard_map(
        body,
        mesh=mesh,
        in_specs=(
            P(("dp", "my"), "mx"),
            P(("dp", "my"), "mx"),
            P(),
            P("my", None, "mx"),
            P("mx", "my"),
            P(),
            P(),
            P(),
            P("dp", "my", "mx"),
            P("dp", "mx", "my"),
            P(("dp", "my"), None),
            P(("dp", "my"), None),
            P("dp", None),
        ),
        out_specs=(
            P(("dp", "my"), "mx"),
            P(("dp", "my"), "mx"),
            P("my", None, "mx"),
            P("mx", "my"),
            P(),
            P(),
            P(),
            P(),
            P("dp", "my", "mx"),
            P("dp", "mx", "my"),
        ),
        check_vma=False,
    )
```

time: 857 us -> 525 us (0.61)
  waiting for transfers between devices: 431 us -> 164 us
  starting transfers between devices: 13 us -> 155 us
  local copies, waits for them, and re-layouts: 158 us -> 31.8 us
  Pallas kernels: 17.3 us -> 122 us
  blocking collectives: 107 us -> 4.59 us
  matrix products: 58.2 us -> 0 us
  other arithmetic: 46.5 us -> 24 us
    all_gather x7 -> x2, waiting for transfers between devices: 193 us -> 0.01 us  [the longest x1 0.01 us: body(): win_full = lax.all_gather(w_in, 'my', axis=1, tiled=True)]
    ppermute x2 -> x72, waiting for transfers between devices: 11 us -> 164 us  [the longest x69 156 us: swap(): lax.ppermute(values, axis, [(i, i ^ step) for i in range(lax.axis_size(ax...]
    ppermute x2 -> x72, starting transfers between devices: 2.93 us -> 155 us  [the longest x69 151 us: swap(): lax.ppermute(values, axis, [(i, i ^ step) for i in range(lax.axis_size(ax...]
    unnamed x21 -> x2, waiting for transfers between devices: 106 us -> 0.7 us
    pallas_call x0 -> x16, Pallas kernels: none -> 104 us  [the longest x2 18.8 us: expert(): pl.pallas_call(lambda *refs: expert_kernel(count, *refs), in_specs=[VMEM]...]
    psum x5 -> x0, blocking collectives: 78.8 us -> none  [the longest x1 40.3 us: body(): lax.psum((full_bias, full_gain_one, full_gain_two, full_router), ('dp', '...]
    reduce_scatter x3 -> x0, waiting for transfers between devices: 78.5 us -> none  [the longest x2 78.1 us: feature_sum(): lax.psum_scatter(values.astype(jnp.bfloat16), 'mx', scatter_dimension=1,...]
    dot_general x15 -> x0, matrix products: 58.2 us -> none  [the longest x1 9.18 us: body(): jnp.einsum('sjcf,sjcd->jfd', activated, back_full, preferred_element_type...]
  transfers between devices with their start and end apart: 20 -> 74, of which waited for: 13 -> 19; matrix products, arithmetic and copies ran while one was open for 21% -> 8% of each run, Pallas kernels for 0% -> 23%
where the time goes in v2:
time: 525 us; the launch traced here: 517 us
  waiting for transfers between devices  164 us (31%)
  starting transfers between devices  155 us (30%)
  Pallas kernels  122 us (23%)
  local copies, waits for them, and re-layouts  31.8 us (6%)
  other arithmetic  24 us (5%)
  between operations  15.6 us (3%)
    ppermute x69, waiting for transfers between devices, swap(): lax.ppermute(values, axis, [(i, i ^ step) for i in range(lax.axis_size(ax...  156 us
    ppermute x69, starting transfers between devices, swap(): lax.ppermute(values, axis, [(i, i ^ step) for i in range(lax.axis_size(ax...  151 us
    pallas_call x2, Pallas kernels, expert(): pl.pallas_call(lambda *refs: expert_kernel(count, *refs), in_specs=[VMEM]...  18.8 us
    unnamed x177, local copies, waits for them, and re-layouts  14.5 us
    pallas_call x1, Pallas kernels, collect(): pl.pallas_call(lambda *refs: collect_kernel(blocks, parts, *refs), grid=(...  13 us
    pallas_call x1, Pallas kernels, enter(): pl.pallas_call(lambda *refs: enter_kernel(parts, *refs), in_specs=[SMEM]...  12.2 us
    pallas_call x2, Pallas kernels, expert_weights(): pl.pallas_call(lambda *refs: expert_weights_kernel(len(rows), *refs), in_...  12.2 us
    pallas_call x1, Pallas kernels, attend_back(): pl.pallas_call(attend_back_kernel, grid=(heads,), in_specs=[pl.BlockSpec(...  11.8 us
  transfers between devices with their start and end apart: 74, of which 19 were waited for; matrix products, arithmetic and copies ran while one was open for 8% of the time, Pallas kernels for 23%

profile of v2, /device:TPU:0, one launch (start us, length us, event | category | flops | bytes accessed | tf_op | source)
XLA Modules:
  0.0 517.4 jit_solution(18247061810605420824)
XLA Ops:
  24.9 15.4 %collective-permute-done.2.refs_3_ = bf16[192,1024]{1,0:T(8,128)(2,1)S(1)} collective-permute-done((bf16[192,1024]{1,0:T(8,128)(2,1)S(1)}, bf16[192,1024]{1,0:T(8,128)(2,1)S(1)}, u32[]{:S(2)}, u32[]{:S(2)}) %collective-permute-start.2) | collective-permute-done | bytes 393248 | tf_op jit(solution)/shard_map/ppermute | solution.py:28
  40.3 33.4 %collective-permute-start.13 = (bf16[192,1024]{1,0:T(8,128)(2,1)}, bf16[192,1024]{1,0:T(8,128)(2,1)}, u32[]{:S(2)}, u32[]{:S(2)}) collective-permute-start(bf16[192,1024]{1,0:T(8,128)(2,1)} %bitcast.9.refs_1_), channel_id=1, source_target_pairs={{0,2},{2,0},{4,6},{6,4},{1,3},{3,1},{5,7},{7,5},{8,10},{10,8},{12,... | collective-permute-start | bytes 1179656 | tf_op jit(solution)/shard_map/ppermute | solution.py:28
  73.7 7.0 %collective-permute-done.1.refs_2_ = bf16[192,1024]{1,0:T(8,128)(2,1)S(1)} collective-permute-done((bf16[192,1024]{1,0:T(8,128)(2,1)S(1)}, bf16[192,1024]{1,0:T(8,128)(2,1)S(1)}, u32[]{:S(2)}, u32[]{:S(2)}) %collective-permute-start.1) | collective-permute-done | bytes 393248 | tf_op jit(solution)/shard_map/ppermute | solution.py:28
  95.0 5.6 %attend.1 = (bf16[192,1024]{1,0:T(8,128)(2,1)S(1)}, f32[3,1,1024]{2,1,0:T(1,128)S(1)}) custom-call(s32[1]{0:T(128)} %bitcast.1.cont_ref.side_ref.refs_0_, bf16[576,1024]{1,0:T(8,128)(2,1)S(1)} %copy-done.2, bf16[576,1024]{1,0:T(8,128)(2,1)S(1)} %copy-done.2, bf16[576,1024]{1,0:T(8,128)(2,1)S(1)} %copy-done.2, ...), custom_call_target="tpu_custom_call" | custom-call | tf_op jit(solution)/shard_map/attend/pallas_call | solution.py:654
  118.2 25.7 %collective-permute-done.8.refs_7_.refs_10_ = bf16[192,768]{1,0:T(8,128)(2,1)S(1)} collective-permute-done((bf16[192,768]{1,0:T(8,128)(2,1)S(1)}, bf16[192,768]{1,0:T(8,128)(2,1)S(1)}, u32[]{:S(2)}, u32[]{:S(2)}) %collective-permute-start.8) | collective-permute-done | bytes 294944 | tf_op jit(solution)/shard_map/ppermute | solution.py:28
  149.9 12.2 %enter.1 = (f32[192,1024]{1,0:T(8,128)}, f32[1,1024]{1,0:T(1,128)S(1)}, bf16[768,1024]{1,0:T(8,128)(2,1)}, f32[2,1024]{1,0:T(2,128)S(1)}, bf16[784,256]{1,0:T(8,...) custom-call(s32[1]{0:T(128)} %bitcast.me_ref.refs_0_, ...), custom_call_target="tpu_custom_call" | custom-call | tf_op jit(solution)/shard_map/enter/pallas_call | solution.py:207
  187.2 16.0 %collective-permute-done.23.refs_2_.refs_3_ = bf16[784,256]{1,0:T(8,128)(2,1)} collective-permute-done((bf16[784,256]{1,0:T(8,128)(2,1)}, bf16[784,256]{1,0:T(8,128)(2,1)}, u32[]{:S(2)}, u32[]{:S(2)}) %collective-permute-start.23) | collective-permute-done | bytes 401440 | tf_op jit(solution)/shard_map/ppermute | solution.py:28
  209.5 9.5 %expert.3 = (bf16[784,256]{1,0:T(8,128)(2,1)S(1)}, bf16[784,256]{1,0:T(8,128)(2,1)S(1)}, bf16[784,256]{1,0:T(8,128)(2,1)S(1)}, bf16[784,256]{1,0:T(8,128)(2,1)S(...) custom-call(bf16[784,256]{1,0:T(8,128)(2,1)S(1)} %copy-done.10, ...), custom_call_target="tpu_custom_call" | custom-call | tf_op jit(solution)/shard_map/expert/pallas_call | solution.py:280
  227.5 8.8 %collective-permute-done.11.refs_2_.refs_3_ = bf16[784,256]{1,0:T(8,128)(2,1)} collective-permute-done((bf16[784,256]{1,0:T(8,128)(2,1)}, bf16[784,256]{1,0:T(8,128)(2,1)}, u32[]{:S(2)}, u32[]{:S(2)}) %collective-permute-start.11) | collective-permute-done | bytes 401440 | tf_op jit(solution)/shard_map/ppermute | solution.py:28
  236.3 9.3 %expert.2 = (bf16[784,256]{1,0:T(8,128)(2,1)S(1)}, bf16[784,256]{1,0:T(8,128)(2,1)}, bf16[784,256]{1,0:T(8,128)(2,1)S(1)}, bf16[784,256]{1,0:T(8,128)(2,1)S(1)},...) custom-call(bf16[784,256]{1,0:T(8,128)(2,1)S(1)} %get-tuple-element.105.refs_0_.refs_1_, ...), custom_call_target="tpu_custom_call" | custom-call | tf_op jit(solution)/shard_map/expert/pallas_call | solution.py:280
  258.8 5.7 %expert_weights.3 = (f32[384,768]{1,0:T(8,128)S(1)}, bf16[384,768]{1,0:T(8,128)(2,1)S(1)}, f32[768,384]{1,0:T(8,128)}, bf16[768,384]{1,0:T(8,128)(2,1)S(1)}) custom-call(s32[1]{0:T(128)} %bitcast.1.cont_ref.side_ref.refs_0_, bf16[784,256]{1,0:T(8,128)(2,1)S(1)} %copy-done.10, bf16[784,256]{1,0:T(8,128)(2,1)S(1)} %copy-done.13, ...), custom_call_target="tpu_custom_call" | custom-call | tf_op jit(solution)/shard_map/expert_weights/pallas_call | solution.py:329
  264.5 12.0 %collective-permute-start.69 = (bf16[384,768]{1,0:T(8,128)(2,1)S(1)}, bf16[384,768]{1,0:T(8,128)(2,1)}, u32[]{:S(2)}, u32[]{:S(2)}) collective-permute-start(bf16[384,768]{1,0:T(8,128)(2,1)S(1)} %get-tuple-element.187), channel_id=1, source_target_pairs={{0,1},{1,0},{2,3},{3,2},{4,5},{5,4},{6,7},{7,6},{8,9},{9,8},{10,11... | collective-permute-start | bytes 1769480 | tf_op jit(solution)/shard_map/ppermute | solution.py:28
  280.0 16.1 %collective-permute-start.71 = (bf16[768,384]{1,0:T(8,128)(2,1)S(1)}, bf16[768,384]{1,0:T(8,128)(2,1)}, u32[]{:S(2)}, u32[]{:S(2)}) collective-permute-start(bf16[768,384]{1,0:T(8,128)(2,1)S(1)} %get-tuple-element.191), channel_id=1, source_target_pairs={{0,1},{1,0},{2,3},{3,2},{4,5},{5,4},{6,7},{7,6},{8,9},{9,8},{10,11... | collective-permute-start | bytes 1769480 | tf_op jit(solution)/shard_map/ppermute | solution.py:28
  296.2 6.5 %expert_weights.2 = (f32[384,768]{1,0:T(8,128)S(1)}, bf16[384,768]{1,0:T(8,128)(2,1)S(1)}, f32[768,384]{1,0:T(8,128)}, bf16[768,384]{1,0:T(8,128)(2,1)}) custom-call(s32[1]{0:T(128)} %bitcast.1.cont_ref.side_ref.refs_0_, bf16[784,256]{1,0:T(8,128)(2,1)S(1)} %get-tuple-element.105.refs_0_.refs_1_, ...), custom_call_target="tpu_custom_call" | custom-call | tf_op jit(solution)/shard_map/expert_weights/pallas_call | solution.py:329
  302.7 9.4 %merge.1 = (bf16[192,1024]{1,0:T(8,128)(2,1)S(1)}, bf16[192,1024]{1,0:T(8,128)(2,1)}, bf16[192,1024]{1,0:T(8,128)(2,1)}, bf16[192,1024]{1,0:T(8,128)(2,1)S(1)}) custom-call(s32[1]{0:T(128)} %bitcast.me_ref.refs_0_, bf16[768,256]{1,0:T(8,128)(2,1)S(1)} %get-tuple-element.114.refs_1_, bf16[768,256]{1,0:T(8,128)(2,1)S(1)} %collective-permute-done.19.refs_2_, ...), custom_call_target="tpu_custom_call" | custom-call | tf_op jit(solution)/shard_map/merge/pallas_call | solution.py:482
  312.9 13.0 %collect.1 = (bf16[768,1024]{1,0:T(8,128)(2,1)}, f32[8,1024]{1,0:T(8,128)S(1)}, f32[8,768]{1,0:T(8,128)S(1)}, bf16[192,1024]{1,0:T(8,128)(2,1)S(1)}, bf16[192,10...) custom-call(bf16[784,256]{1,0:T(8,128)(2,1)S(1)} %get-tuple-element.136.refs_0_, ...), custom_call_target="tpu_custom_call" | custom-call | tf_op jit(solution)/shard_map/collect/pallas_call | solution.py:378
  340.6 26.1 %collective-permute-done.44.refs_7_ = f32[8,1024]{1,0:T(8,128)S(1)} collective-permute-done((f32[8,1024]{1,0:T(8,128)S(1)}, f32[8,1024]{1,0:T(8,128)S(1)}, u32[]{:S(2)}, u32[]{:S(2)}) %collective-permute-start.44) | collective-permute-done | bytes 32800 | tf_op jit(solution)/shard_map/ppermute | solution.py:28
  369.2 7.6 %turn.1 = (bf16[192,1024]{1,0:T(8,128)(2,1)S(1)}, bf16[768,1024]{1,0:T(8,128)(2,1)}, f32[192,1024]{1,0:T(8,128)S(1)}, f32[8,768]{1,0:T(8,128)S(1)}, f32[8,768]{1,0:T(8,128)S(1)}) custom-call(s32[1]{0:T(128)} %bitcast.me_ref.refs_0_, bf16[192,1024]{1,0:T(8,128)(2,1)S(1)} %get-tuple-element.146.refs_1_, bf16[192,1024]{1,0:T(8,128)(2,1)S(1)} %collective-permute-done.40.refs_2_, ...), custom_call_target="tpu_custom_call" | custom-call | tf_op jit(solution)/shard_map/turn/pallas_call | solution.py:440
  377.4 11.8 %attend_back.1 = (bf16[192,1024]{1,0:T(8,128)(2,1)S(1)}, bf16[192,1024]{1,0:T(8,128)(2,1)S(1)}, bf16[192,1024]{1,0:T(8,128)(2,1)S(1)}, bf16[192,1024]{1,0:T(8,12...) custom-call(s32[1]{0:T(128)} %bitcast.1.cont_ref.side_ref.refs_0_, ...), custom_call_target="tpu_custom_call" | custom-call | tf_op jit(solution)/shard_map/attend_back/pallas_call | solution.py:769
  398.8 6.5 %collective-permute-done.46.refs_4_ = bf16[192,1024]{1,0:T(8,128)(2,1)S(1)} collective-permute-done((bf16[192,1024]{1,0:T(8,128)(2,1)}, bf16[192,1024]{1,0:T(8,128)(2,1)S(1)}, u32[]{:S(2)}, u32[]{:S(2)}) %collective-permute-start.46) | collective-permute-done | bytes 393248 | tf_op jit(solution)/shard_map/ppermute | solution.py:923
  406.7 6.5 %leave.1 = (bf16[576,1024]{1,0:T(8,128)(2,1)}, f32[8,1024]{1,0:T(8,128)S(1)}, f32[8,768]{1,0:T(8,128)S(1)}, bf16[192,1024]{1,0:T(8,128)(2,1)S(1)}, bf16[192,1024...) custom-call(s32[1]{0:T(128)} %bitcast.me_ref.refs_0_, ...), custom_call_target="tpu_custom_call" | custom-call | tf_op jit(solution)/shard_map/leave/pallas_call | solution.py:545
  442.7 6.4 %collective-permute-done.67 = f32[11,768]{1,0:T(8,128)S(1)} collective-permute-done((f32[11,768]{1,0:T(8,128)S(1)}, f32[11,768]{1,0:T(8,128)S(1)}, u32[]{:S(2)}, u32[]{:S(2)}) %collective-permute-start.67) | collective-permute-done | bytes 33824 | tf_op jit(solution)/shard_map/ppermute | solution.py:28
  466.2 19.7 %collective-permute-done.59 = bf16[192,384]{1,0:T(8,128)(2,1)} collective-permute-done((bf16[192,384]{1,0:T(8,128)(2,1)S(1)}, bf16[192,384]{1,0:T(8,128)(2,1)}, u32[]{:S(2)}, u32[]{:S(2)}) %collective-permute-start.59) | collective-permute-done | bytes 147488 | tf_op jit(solution)/shard_map/ppermute | solution.py:28
  502.0 6.7 %collective-permute-done.56 = bf16[384,576]{1,0:T(8,128)(2,1)S(1)} collective-permute-done((bf16[384,576]{1,0:T(8,128)(2,1)S(1)}, bf16[384,576]{1,0:T(8,128)(2,1)S(1)}, u32[]{:S(2)}, u32[]{:S(2)}) %collective-permute-start.56) | collective-permute-done | bytes 442400 | tf_op jit(solution)/shard_map/ppermute | solution.py:28
  (381 shorter events, 205.0 us)
Async XLA Ops:
  7.2 176.8 %all-gather.3.cloned.1.call-start = ((), (), s32[]{:S(2)}) async-start(), calls=%async_computation | async-start | bytes 3538944 | tf_op jit(solution)/shard_map/all_gather | solution.py:865
  8.0 197.2 %all-gather.5.cloned.1.call-start = ((), (), s32[]{:S(2)}) async-start(), calls=%async_computation.1 | async-start | bytes 3538944 | tf_op jit(solution)/shard_map/all_gather | solution.py:866
  8.0 93.9 %collective-permute-start.15 = (bf16[192,1024]{1,0:T(8,128)(2,1)}, bf16[192,1024]{1,0:T(8,128)(2,1)}, u32[]{:S(2)}, u32[]{:S(2)}) collective-permute-start(bf16[192,1024]{1,0:T(8,128)(2,1)} %bitcast.9.refs_1_), channel_id=1, source_target_pairs={{0,6},{2,4},{4,2},{6,0},{1,7},{3,5},{5,3},{7,1},{8,14},{10,12},{12... | collective-permute-start | bytes 1179656 | tf_op jit(solution)/shard_map/ppermute | solution.py:28
  13.1 92.0 %collective-permute-start.14 = (bf16[192,1024]{1,0:T(8,128)(2,1)}, bf16[192,1024]{1,0:T(8,128)(2,1)}, u32[]{:S(2)}, u32[]{:S(2)}) collective-permute-start(bf16[192,1024]{1,0:T(8,128)(2,1)} %bitcast.9.refs_1_), channel_id=1, source_target_pairs={{0,4},{2,6},{4,0},{6,2},{1,5},{3,7},{5,1},{7,3},{8,12},{10,14},{12... | collective-permute-start | bytes 1179656 | tf_op jit(solution)/shard_map/ppermute | solution.py:28
  15.0 65.7 %collective-permute-start.1 = (bf16[192,1024]{1,0:T(8,128)(2,1)S(1)}, bf16[192,1024]{1,0:T(8,128)(2,1)S(1)}, u32[]{:S(2)}, u32[]{:S(2)}) collective-permute-start(bf16[192,1024]{1,0:T(8,128)(2,1)S(1)} %bitcast.42), channel_id=1, source_target_pairs={{0,4},{2,6},{4,0},{6,2},{1,5},{3,7},{5,1},{7,3},{8,12},{10,14},{12... | collective-permute-start | bytes 1179656 | tf_op jit(solution)/shard_map/ppermute | solution.py:28
  16.1 67.3 %collective-permute-start = (bf16[192,1024]{1,0:T(8,128)(2,1)S(1)}, bf16[192,1024]{1,0:T(8,128)(2,1)}, u32[]{:S(2)}, u32[]{:S(2)}) collective-permute-start(bf16[192,1024]{1,0:T(8,128)(2,1)S(1)} %bitcast.43), channel_id=1, source_target_pairs={{0,2},{2,0},{4,6},{6,4},{1,3},{3,1},{5,7},{7,5},{8,10},{10,8},{12,... | collective-permute-start | bytes 1179656 | tf_op jit(solution)/shard_map/ppermute | solution.py:28
  40.3 64.9 %collective-permute-start.13 = (bf16[192,1024]{1,0:T(8,128)(2,1)}, bf16[192,1024]{1,0:T(8,128)(2,1)}, u32[]{:S(2)}, u32[]{:S(2)}) collective-permute-start(bf16[192,1024]{1,0:T(8,128)(2,1)} %bitcast.9.refs_1_), channel_id=1, source_target_pairs={{0,2},{2,0},{4,6},{6,4},{1,3},{3,1},{5,7},{7,5},{8,10},{10,8},{12,... | collective-permute-start | bytes 1179656 | tf_op jit(solution)/shard_map/ppermute | solution.py:28
  100.6 46.4 %collective-permute-start.6 = (bf16[192,1024]{1,0:T(8,128)(2,1)S(1)}, bf16[192,1024]{1,0:T(8,128)(2,1)S(1)}, u32[]{:S(2)}, u32[]{:S(2)}) collective-permute-start(bf16[192,1024]{1,0:T(8,128)(2,1)S(1)} %get-tuple-element.102.refs_1_.o_ref), channel_id=1, source_target_pairs={{0,6},{2,4},{4,2},{6,0},{1,7},{3,5},{5,3},{7,1},{8,14},{10,12},{12... | collective-permute-start | bytes 1179656 | tf_op jit(solution)/shard_map/ppermute | solution.py:28
  101.9 45.1 %collective-permute-start.5 = (bf16[192,1024]{1,0:T(8,128)(2,1)S(1)}, bf16[192,1024]{1,0:T(8,128)(2,1)S(1)}, u32[]{:S(2)}, u32[]{:S(2)}) collective-permute-start(bf16[192,1024]{1,0:T(8,128)(2,1)S(1)} %get-tuple-element.102.refs_1_.o_ref), channel_id=1, source_target_pairs={{0,4},{2,6},{4,0},{6,2},{1,5},{3,7},{5,1},{7,3},{8,12},{10,14},{12... | collective-permute-start | bytes 1179656 | tf_op jit(solution)/shard_map/ppermute | solution.py:28
  101.9 45.1 %collective-permute-start.4 = (bf16[192,1024]{1,0:T(8,128)(2,1)S(1)}, bf16[192,1024]{1,0:T(8,128)(2,1)S(1)}, u32[]{:S(2)}, u32[]{:S(2)}) collective-permute-start(bf16[192,1024]{1,0:T(8,128)(2,1)S(1)} %get-tuple-element.102.refs_1_.o_ref), channel_id=1, source_target_pairs={{0,2},{2,0},{4,6},{6,4},{1,3},{3,1},{5,7},{7,5},{8,10},{10,8},{12,... | collective-permute-start | bytes 1179656 | tf_op jit(solution)/shard_map/ppermute | solution.py:28
  105.2 40.3 %collective-permute-start.7 = (bf16[192,768]{1,0:T(8,128)(2,1)S(1)}, bf16[192,768]{1,0:T(8,128)(2,1)S(1)}, u32[]{:S(2)}, u32[]{:S(2)}) collective-permute-start(bf16[192,768]{1,0:T(8,128)(2,1)S(1)} %all_gather.13.refs_5_.refs_8_.refs_9_), channel_id=1, source_target_pairs={{0,2},{2,0},{4,6},{6,4},{1,3},{3,1},{5,7},{7,5},{8,10},{10,8},{12,... | collective-permute-start | bytes 884744 | tf_op jit(solution)/shard_map/ppermute | solution.py:28
  174.4 48.2 %collective-permute-start.17 = (bf16[768,256]{1,0:T(8,128)(2,1)}, bf16[768,256]{1,0:T(8,128)(2,1)}, u32[]{:S(2)}, u32[]{:S(2)}) collective-permute-start(bf16[768,256]{1,0:T(8,128)(2,1)} %get-tuple-element.111), channel_id=1, source_target_pairs={{0,16},{8,24},{16,0},{24,8},{1,17},{9,25},{17,1},{25,9},{2,18},{10... | collective-permute-start | bytes 1179656 | tf_op jit(solution)/shard_map/ppermute | solution.py:28
  182.1 42.1 %collective-permute-start.18 = (bf16[768,256]{1,0:T(8,128)(2,1)}, bf16[768,256]{1,0:T(8,128)(2,1)}, u32[]{:S(2)}, u32[]{:S(2)}) collective-permute-start(bf16[768,256]{1,0:T(8,128)(2,1)} %get-tuple-element.112), channel_id=1, source_target_pairs={{0,24},{8,16},{16,8},{24,0},{1,25},{9,17},{17,9},{25,1},{2,26},{10... | collective-permute-start | bytes 1179656 | tf_op jit(solution)/shard_map/ppermute | solution.py:28
  183.5 42.9 %collective-permute-start.10 = (bf16[784,256]{1,0:T(8,128)(2,1)}, bf16[784,256]{1,0:T(8,128)(2,1)S(1)}, u32[]{:S(2)}, u32[]{:S(2)}) collective-permute-start(bf16[784,256]{1,0:T(8,128)(2,1)} %get-tuple-element.106), channel_id=1, source_target_pairs={{0,8},{8,0},{16,24},{24,16},{1,9},{9,1},{17,25},{25,17},{2,10},{10... | collective-permute-start | bytes 1204232 | tf_op jit(solution)/shard_map/ppermute | solution.py:28
  264.5 61.6 %collective-permute-start.69 = (bf16[384,768]{1,0:T(8,128)(2,1)S(1)}, bf16[384,768]{1,0:T(8,128)(2,1)}, u32[]{:S(2)}, u32[]{:S(2)}) collective-permute-start(bf16[384,768]{1,0:T(8,128)(2,1)S(1)} %get-tuple-element.187), channel_id=1, source_target_pairs={{0,1},{1,0},{2,3},{3,2},{4,5},{5,4},{6,7},{7,6},{8,9},{9,8},{10,11... | collective-permute-start | bytes 1769480 | tf_op jit(solution)/shard_map/ppermute | solution.py:28
  280.0 52.8 %collective-permute-start.71 = (bf16[768,384]{1,0:T(8,128)(2,1)S(1)}, bf16[768,384]{1,0:T(8,128)(2,1)}, u32[]{:S(2)}, u32[]{:S(2)}) collective-permute-start(bf16[768,384]{1,0:T(8,128)(2,1)S(1)} %get-tuple-element.191), channel_id=1, source_target_pairs={{0,1},{1,0},{2,3},{3,2},{4,5},{5,4},{6,7},{7,6},{8,9},{9,8},{10,11... | collective-permute-start | bytes 1769480 | tf_op jit(solution)/shard_map/ppermute | solution.py:28
  326.1 40.6 %collective-permute-start.40 = (bf16[192,1024]{1,0:T(8,128)(2,1)S(1)}, bf16[192,1024]{1,0:T(8,128)(2,1)S(1)}, u32[]{:S(2)}, u32[]{:S(2)}) collective-permute-start(bf16[192,1024]{1,0:T(8,128)(2,1)S(1)} %get-tuple-element.147), channel_id=1, source_target_pairs={{0,2},{2,0},{4,6},{6,4},{1,3},{3,1},{5,7},{7,5},{8,10},{10,8},{12,... | collective-permute-start | bytes 1179656 | tf_op jit(solution)/shard_map/ppermute | solution.py:28
  326.2 43.1 %collective-permute-start.41 = (bf16[192,1024]{1,0:T(8,128)(2,1)S(1)}, bf16[192,1024]{1,0:T(8,128)(2,1)S(1)}, u32[]{:S(2)}, u32[]{:S(2)}) collective-permute-start(bf16[192,1024]{1,0:T(8,128)(2,1)S(1)} %get-tuple-element.148), channel_id=1, source_target_pairs={{0,4},{2,6},{4,0},{6,2},{1,5},{3,7},{5,1},{7,3},{8,12},{10,14},{12... | collective-permute-start | bytes 1179656 | tf_op jit(solution)/shard_map/ppermute | solution.py:28
  366.7 50.9 %collective-permute-start.70 = (bf16[768,384]{1,0:T(8,128)(2,1)}, bf16[768,384]{1,0:T(8,128)(2,1)}, u32[]{:S(2)}, u32[]{:S(2)}) collective-permute-start(bf16[768,384]{1,0:T(8,128)(2,1)} %get-tuple-element.189), channel_id=1, source_target_pairs={{0,1},{1,0},{2,3},{3,2},{4,5},{5,4},{6,7},{7,6},{8,9},{9,8},{10,11... | collective-permute-start | bytes 1769480 | tf_op jit(solution)/shard_map/ppermute | solution.py:28
  366.7 66.7 %collective-permute-start.31 = (bf16[192,1024]{1,0:T(8,128)(2,1)}, bf16[192,1024]{1,0:T(8,128)(2,1)}, u32[]{:S(2)}, u32[]{:S(2)}) collective-permute-start(bf16[192,1024]{1,0:T(8,128)(2,1)} %get-tuple-element.133), channel_id=1, source_target_pairs={{0,2},{2,0},{4,6},{6,4},{1,3},{3,1},{5,7},{7,5},{8,10},{10,8},{12,... | collective-permute-start | bytes 1179656 | tf_op jit(solution)/shard_map/ppermute | solution.py:28
  366.7 66.7 %collective-permute-start.32 = (bf16[192,1024]{1,0:T(8,128)(2,1)}, bf16[192,1024]{1,0:T(8,128)(2,1)}, u32[]{:S(2)}, u32[]{:S(2)}) collective-permute-start(bf16[192,1024]{1,0:T(8,128)(2,1)} %get-tuple-element.134), channel_id=1, source_target_pairs={{0,4},{2,6},{4,0},{6,2},{1,5},{3,7},{5,1},{7,3},{8,12},{10,14},{12... | collective-permute-start | bytes 1179656 | tf_op jit(solution)/shard_map/ppermute | solution.py:28
  439.4 60.5 %collective-permute-start.51 = (bf16[192,1024]{1,0:T(8,128)(2,1)}, bf16[192,1024]{1,0:T(8,128)(2,1)S(1)}, u32[]{:S(2)}, u32[]{:S(2)}) collective-permute-start(bf16[192,1024]{1,0:T(8,128)(2,1)} %get-tuple-element.165), channel_id=1, source_target_pairs={{0,2},{2,0},{4,6},{6,4},{1,3},{3,1},{5,7},{7,5},{8,10},{10,8},{12,... | collective-permute-start | bytes 1179656 | tf_op jit(solution)/shard_map/ppermute | solution.py:28
  440.7 47.9 %collective-permute-start.54 = (bf16[384,576]{1,0:T(8,128)(2,1)S(1)}, bf16[384,576]{1,0:T(8,128)(2,1)}, u32[]{:S(2)}, u32[]{:S(2)}) collective-permute-start(bf16[384,576]{1,0:T(8,128)(2,1)S(1)} %get-tuple-element.170), channel_id=1, source_target_pairs={{0,1},{1,0},{2,3},{3,2},{4,5},{5,4},{6,7},{7,6},{8,9},{9,8},{10,11... | collective-permute-start | bytes 1327112 | tf_op jit(solution)/shard_map/ppermute | solution.py:28
  460.3 39.6 %collective-permute-start.52 = (bf16[192,1024]{1,0:T(8,128)(2,1)S(1)}, bf16[192,1024]{1,0:T(8,128)(2,1)S(1)}, u32[]{:S(2)}, u32[]{:S(2)}) collective-permute-start(bf16[192,1024]{1,0:T(8,128)(2,1)S(1)} %copy-done.56), channel_id=1, source_target_pairs={{0,4},{2,6},{4,0},{6,2},{1,5},{3,7},{5,1},{7,3},{8,12},{10,14},{12... | collective-permute-start | bytes 1179656 | tf_op jit(solution)/shard_map/ppermute | solution.py:28
  (138 other events, 2027.4 us)
Sparse Core Ops, SparseCore 0:
  9.6 13.6 all-gather.2
  24.8 12.2 all-gather.4
